TPU v7x, 256 devices: a whole 4x4x8 slice. The times are simulated.
256 devices in a mesh: gx: 4 (over y), gy: 8 (over x, core), gz: 8 (over z).
Axes of the slice: x: 4, y: 4, z: 8, core: 2. Of those that a mesh axis runs over, the one named last changes fastest.
Arguments:
- displacement: float32 [3, 64, 128, 1024], P(None, 'gx', 'gy', 'gz'), may hold values from -0.15 to 0.15
- zone_mass: float32 [64, 128, 1024], P('gx', 'gy', 'gz'), may hold values from 0.5 to 2
- zone_energy: float32 [64, 128, 1024], P('gx', 'gy', 'gz'), may hold values from 0.2 to 5
- slave_position: float32 [65536, 3, 128], P(('gx', 'gy', 'gz')), may hold values from -3 to 3
- slave_stiffness: float32 [65536, 128], P(('gx', 'gy', 'gz')), may hold values from 0.05 to 0.5
- slave_active: int32 [65536, 128], P(('gx', 'gy', 'gz')), may hold values 0 or 1
- partner_peer: int32 [65536, 1], P(('gx', 'gy', 'gz')), may hold values from 0 to 63; in each aligned block of 256 rows (0 to 255, 256 to 511, ...) at most 8 rows name the same one
- partner_block: int32 [65536, 1], P(('gx', 'gy', 'gz')), may hold values from 0 to 63
- master_node: int32 [16384, 128], P(('gx', 'gy', 'gz')), may hold values from 0 to 32767
- master_area: float32 [16384, 3, 128], P(('gx', 'gy', 'gz')), may hold values from -3.6 to 3.6
- face_active: int32 [16384, 128], P(('gx', 'gy', 'gz')), may hold values 0 or 1
Outputs:
- node_force: float32 [3, 64, 128, 1024], P(None, 'gx', 'gy', 'gz')
- slave_force: float32 [65536, 3, 128], P(('gx', 'gy', 'gz'))
Inputs may be any that keep to these rules, and one draw needn't show every extreme that they name: `partner_peer`: among the slave blocks of one device, at most 8 name the same partition, and in some devices exactly 8 do. `master_node`: indices repeat freely.
All inputs are finite; a program needn't handle non-finite values. No bound on the sum of `slave_active` or of `face_active` on one device may be relied on, other than what follows from the above.
Results may differ from a plain program's by a relative error of at most 0.000094.
Values sent between devices are 32-bit elements; how exact they have to be, the bound alone decides.
A program may use at most 128 MiB of HBM per device.

v0:
```python
import jax
import jax.numpy as jnp
from jax import lax
from jax.sharding import PartitionSpec as P

gamma_gas = 5.0 / 3.0
corner_offsets = [
    (0, 0, 0),
    (0, 0, 1),
    (0, 1, 0),
    (0, 1, 1),
    (1, 0, 0),
    (1, 0, 1),
    (1, 1, 0),
    (1, 1, 1),
]


def extended_2(cells, sides, width):
    for axis, dim in sides:
        count = lax.axis_size(axis)
        ends = count - 1
        head = lax.slice_in_dim(cells, 0, width, axis=dim)
        tail = lax.slice_in_dim(cells, cells.shape[dim] - width, cells.shape[dim], axis=dim)
        cells = jnp.concatenate(
            [
                lax.ppermute(tail, axis, [(i, (i + 1) % count) for i in range(ends)]),
                cells,
                lax.ppermute(head, axis, [((i + 1) % count, i) for i in range(ends)]),
            ],
            axis=dim,
        )
    return cells


def cross_parts(left, right):
    return [
        left[1] * right[2] - left[2] * right[1],
        left[2] * right[0] - left[0] * right[2],
        left[0] * right[1] - left[1] * right[0],
    ]


def zone_state(corner_moves, masses, energies, valid):
    edges = []
    for axis_pick in range(3):
        parts = []
        for comp in range(3):
            total = jnp.zeros_like(masses)
            for moved, offset in zip(corner_moves, corner_offsets):
                total = total + (2.0 * offset[axis_pick] - 1.0) * moved[comp]
            total = total * 0.25
            if comp == axis_pick:
                total = total + 1.0
            parts.append(total)
        edges.append(parts)
    cross_yz = cross_parts(edges[1], edges[2])
    cross_zx = cross_parts(edges[2], edges[0])
    cross_xy = cross_parts(edges[0], edges[1])
    volume = edges[0][0] * cross_yz[0] + edges[0][1] * cross_yz[1] + edges[0][2] * cross_yz[2]
    pressure = jnp.where(
        valid, (gamma_gas - 1.0) * masses * energies / jnp.where(valid, volume, 1.0), 0.0
    )
    return (pressure, cross_yz, cross_zx, cross_xy)


def corner_force(state, offset):
    pressure, cross_yz, cross_zx, cross_xy = state
    sign_x = 2.0 * offset[0] - 1.0
    sign_y = 2.0 * offset[1] - 1.0
    sign_z = 2.0 * offset[2] - 1.0
    return jnp.stack(
        [
            pressure
            * 0.25
            * (sign_x * cross_yz[comp] + sign_y * cross_zx[comp] + sign_z * cross_xy[comp])
            for comp in range(3)
        ]
    )


def contact_block(position, stiffness, centers, areas, active):
    center_dot = centers[0] * areas[0] + centers[1] * areas[1] + centers[2] * areas[2]
    signed_gap = (
        position[0][:, None] * areas[0][None, :]
        + position[1][:, None] * areas[1][None, :]
        + position[2][:, None] * areas[2][None, :]
        - center_dot[None, :]
    )
    intersection = jnp.maximum(-signed_gap, 0.0) * active[None, :]
    slave_push = stiffness[None, :] * jnp.dot(
        areas, intersection.T, precision=lax.Precision.HIGHEST
    )
    face_push = -areas * jnp.dot(stiffness, intersection, precision=lax.Precision.HIGHEST)[None, :]
    return (slave_push, face_push)


def axis_valid(position, count, length):
    global_row = position * count + jnp.arange(count + 1, dtype=jnp.int32) - 1
    return (global_row >= 0) & (global_row <= length - 2)


def body(
    displacement,
    zone_mass,
    zone_energy,
    slave_position,
    slave_stiffness,
    slave_active,
    partner_peer,
    partner_block,
    master_node,
    master_area,
    face_active,
):
    cells_x, cells_y, cells_z = (
        displacement.shape[1],
        displacement.shape[2],
        displacement.shape[3],
    )
    fields = jnp.concatenate([displacement, zone_mass[None], zone_energy[None]], axis=0)
    extended = extended_2(fields, (("gx", 1), ("gy", 2), ("gz", 3)), 1)
    valid_x = axis_valid(lax.axis_index("gx"), cells_x, cells_x * lax.axis_size("gx"))
    valid_y = axis_valid(lax.axis_index("gy"), cells_y, cells_y * lax.axis_size("gy"))
    valid_z = axis_valid(lax.axis_index("gz"), cells_z, cells_z * lax.axis_size("gz"))
    valid = valid_x[:, None, None] & valid_y[None, :, None] & valid_z[None, None, :]
    corner_moves = [
        extended[0:3, a : a + cells_x + 1, b : b + cells_y + 1, e : e + cells_z + 1]
        for a, b, e in corner_offsets
    ]
    masses = extended[3, : cells_x + 1, : cells_y + 1, : cells_z + 1]
    energies = extended[4, : cells_x + 1, : cells_y + 1, : cells_z + 1]
    state = zone_state(corner_moves, masses, energies, valid)
    node_force = jnp.zeros((3, cells_x, cells_y, cells_z), jnp.float32)
    for offset in corner_offsets:
        a, b, e = offset
        forces = corner_force(state, offset)
        node_force = (
            node_force
            + forces[:, 1 - a : 1 - a + cells_x, 1 - b : 1 - b + cells_y, 1 - e : 1 - e + cells_z]
        )
    slave_count = slave_position.shape[0]
    block_width = slave_position.shape[2]
    master_count = master_area.shape[0]
    size_y = lax.axis_size("gy")
    size_z = lax.axis_size("gz")
    peers = size_y * size_z
    slots = max(2, 2 * slave_count // peers)
    total_slots = peers * slots
    stiffness = slave_stiffness * slave_active.astype(jnp.float32)
    payload = jnp.concatenate([slave_position, stiffness[:, None, :]], axis=1).reshape(
        slave_count, 4 * block_width
    )
    target = partner_peer[:, 0]
    one_hot = (target[:, None] == jnp.arange(peers, dtype=jnp.int32)[None, :]).astype(jnp.int32)
    earlier = jnp.cumsum(one_hot, axis=0) - one_hot
    slot_of = jnp.sum(earlier * one_hot, axis=1)
    place = target * slots + slot_of
    place_hits = place[:, None] == jnp.arange(total_slots, dtype=jnp.int32)[None, :]
    send_table = place_hits.astype(jnp.float32)
    outgoing = jnp.dot(send_table.T, payload, precision=lax.Precision.HIGHEST).reshape(
        peers, slots, 4, block_width
    )
    block_ids = jnp.sum(
        place_hits.astype(jnp.int32) * partner_block[:, 0][:, None], axis=0
    ).reshape(peers, slots)
    arrived, arrived_ids = (
        lax.all_to_all(outgoing, ("gy", "gz"), split_axis=0, concat_axis=0, tiled=True),
        lax.all_to_all(block_ids, ("gy", "gz"), split_axis=0, concat_axis=0, tiled=True),
    )
    arrived = arrived.reshape(total_slots, 4, block_width)
    arrived_ids = arrived_ids.reshape(total_slots)
    flat_moves = displacement.reshape(3, -1)
    centers = jnp.transpose(flat_moves[:, master_node], (1, 0, 2))
    face_live = face_active.astype(jnp.float32)
    master_pack = jnp.concatenate([centers, master_area, face_live[:, None, :]], axis=1).reshape(
        master_count, 7 * block_width
    )
    owner_table = (
        arrived_ids[:, None] == jnp.arange(master_count, dtype=jnp.int32)[None, :]
    ).astype(jnp.float32)
    slot_pack = jnp.dot(owner_table, master_pack, precision=lax.Precision.HIGHEST).reshape(
        total_slots, 7, block_width
    )
    groups = total_slots // 32

    def per_group(items):
        position, stiff_rows, center_rows, area_rows, live_rows = items
        return jax.vmap(contact_block)(position, stiff_rows, center_rows, area_rows, live_rows)

    pushes, face_terms = lax.map(
        per_group,
        (
            arrived[:, 0:3].reshape(groups, 32, 3, block_width),
            arrived[:, 3].reshape(groups, 32, block_width),
            slot_pack[:, 0:3].reshape(groups, 32, 3, block_width),
            slot_pack[:, 3:6].reshape(groups, 32, 3, block_width),
            slot_pack[:, 6].reshape(groups, 32, block_width),
        ),
    )
    pushes = pushes.reshape(peers, slots, 3, block_width)
    face_terms = face_terms.reshape(total_slots, 3 * block_width)
    returned = lax.all_to_all(pushes, ("gy", "gz"), split_axis=0, concat_axis=0, tiled=True)
    slave_force = jnp.dot(
        send_table, returned.reshape(total_slots, 3 * block_width), precision=lax.Precision.HIGHEST
    ).reshape(slave_count, 3, block_width)
    reactions = jnp.dot(owner_table.T, face_terms, precision=lax.Precision.HIGHEST).reshape(
        master_count, 3, block_width
    )
    reaction_flat = jnp.transpose(reactions, (1, 0, 2)).reshape(3, -1)
    total_flat = node_force.reshape(3, -1).at[:, master_node.reshape(-1)].add(reaction_flat)
    return (total_flat.reshape(3, cells_x, cells_y, cells_z), slave_force)


def solution(mesh):
    return jax.shard_map(
        body,
        mesh=mesh,
        in_specs=(
            P(None, "gx", "gy", "gz"),
            P("gx", "gy", "gz"),
            P("gx", "gy", "gz"),
            P(("gx", "gy", "gz"), None, None),
            P(("gx", "gy", "gz"), None),
            P(("gx", "gy", "gz"), None),
            P(("gx", "gy", "gz"), None),
            P(("gx", "gy", "gz"), None),
            P(("gx", "gy", "gz"), None),
            P(("gx", "gy", "gz"), None, None),
            P(("gx", "gy", "gz"), None),
        ),
        out_specs=(P(None, "gx", "gy", "gz"), P(("gx", "gy", "gz"), None, None)),
        check_vma=False,
    )
```

profile of v0, /device:TPU:1, one launch (start us, length us, event | category | flops | bytes accessed | tf_op | source)
XLA Modules:
  0.0 463.6 jit_solution(6944498911715461854)
XLA Ops:
  1.5 4.0 collective-permute-start
  11.4 12.4 %all-to-all-start = ((s32[64,1,8]{2,1,0:T(1,128)}), s32[64,1,8]{2,1,0:T(1,128)S(1)}, u32[]{:S(2)}, u32[]{:S(2)}) async-start(s32[64,1,8]{2,1,0:T(1,128)} %bitcast.28), calls=%async_computation | async-start | bytes 65536 | tf_op jit(solution)/shard_map/all_to_all | solution.py:169
  28.7 4.3 all-to-all-done
  33.0 6.2 %all-to-all-start.1 = ((f32[64,8,4,128]{3,1,2,0:T(8,128)}), f32[64,8,4,128]{3,1,2,0:T(8,128)}, u32[]{:S(2)}, u32[]{:S(2)}) async-start(f32[64,8,4,128]{3,1,2,0:T(8,128)} %fusion.29), calls=%async_computation.1 | async-start | bytes 2097152 | tf_op jit(solution)/shard_map/all_to_all | solution.py:168
  39.3 8.5 %copy.125 = f32[3,16,16,128]{0,3,2,1:T(8,128)} copy(f32[3,16,16,128]{3,2,1,0:T(8,128)S(1)} %copy-done.1) | data formatting | bytes 786432 | tf_op args[0]
  47.8 33.6 %gather_fusion = f32[8192,3]{1,0:T(8,128)} fusion(f32[3,32768]{0,1:T(8,128)} %bitcast.176, s32[8192]{0:T(1024)S(1)} %fusion.91), kind=kCustom, calls=%fused_computation | custom fusion | bytes 229376 | tf_op jit(solution)/shard_map/gather | solution.py:174
  92.3 5.0 %copy.112 = f32[5,18,16,128]{2,1,3,0:T(8,128)} copy(f32[5,18,16,128]{3,2,1,0:T(8,128)S(1)} %pad_maximum_fusion.1) | data formatting | bytes 1474560 | tf_op jit(solution)/shard_map/concatenate | solution.py:25
  97.3 4.8 %copy.111 = f32[5,18,1,128]{2,1,3,0:T(8,128)} copy(f32[5,18,1,128]{3,1,2,0:T(8,128)S(1)} %collective-permute-done.2) | data formatting | bytes 92160 | tf_op jit(solution)/shard_map/ppermute | solution.py:27
  102.1 4.8 %copy.113 = f32[5,18,1,128]{2,1,3,0:T(8,128)} copy(f32[5,18,1,128]{3,1,2,0:T(8,128)S(1)} %collective-permute-done.3) | data formatting | bytes 92160 | tf_op jit(solution)/shard_map/ppermute | solution.py:29
  106.9 9.9 %pad_maximum_fusion = f32[5,18,18,128]{2,1,3,0:T(8,128)S(1)} fusion(f32[5,18,1,128]{2,1,3,0:T(8,128)} %copy.113, f32[5,18,16,128]{2,1,3,0:T(8,128)} %copy.112, f32[5,18,1,128]{2,1,3,0:T(8,128)} %copy.111), kind=kLoop, calls=%fused_computation.46 | loop fusion | flops 414720 | bytes 1658880 | tf_op jit(solution)/shard_map/concatenate | solution.py:25
  126.5 5.2 %copy.115 = f32[5,18,18,128]{3,2,1,0:T(8,128)S(1)} copy(f32[5,18,18,128]{2,1,3,0:T(8,128)} %copy-done) | data formatting | bytes 1658880 | tf_op jit(solution)/shard_map/concatenate | solution.py:25
  137.1 225.1 %while.12 = (s32[]{:T(128)}, f32[16,32,3,128]{3,2,1,0:T(4,128)}, f32[16,32,3,128]{3,2,1,0:T(4,128)}, f32[16,32,128]{2,1,0:T(8,128)}, f32[16,32,3,128]{3,1,0,2:T(...) while((s32[]{:T(128)}, f32[16,32,3,128]{3,2,1,0:T(4,128)}, ...), condition=%wide.region_5.6_spmd, body=%wide.region_4.5_spmd.sunk | while | flops 34660352 | bytes 1410161 | solution.py:191
  140.3 3.7 fusion.112
  145.4 5.7 %fusion.111 = f32[16,32,3,128]{3,2,1,0:T(4,128)} fusion(f32[16,32,3,128]{3,2,1,0:T(4,128)} %get-tuple-element.281, s32[]{:T(128)} %get-tuple-element.280, f32[32,128]{1,0:T(8,128)S(1)} %dynamic-slice_bitcast_fusion.4, f32[32,128]{1,0:T(8,128)S(1)} %bitcast.198, f32[32,128]{1,0:T(8,128)S(1)} %bitcast.200, f32[32,128]{1,0:T(8,128)S(1)} %get-tuple-element.266, ...), kind=kOutput, calls=%fused_computation.7.clone.1 | convolution fusion | flops 23605248 | bytes 262656 | tf_op jit(solution)/shard_map/while/body/eval_jaxpr/vmap()/dot_general | solution.py:91
  154.4 3.7 fusion.112
  159.5 5.7 %fusion.111 = f32[16,32,3,128]{3,2,1,0:T(4,128)} fusion(f32[16,32,3,128]{3,2,1,0:T(4,128)} %get-tuple-element.281, s32[]{:T(128)} %get-tuple-element.280, f32[32,128]{1,0:T(8,128)S(1)} %dynamic-slice_bitcast_fusion.4, f32[32,128]{1,0:T(8,128)S(1)} %bitcast.198, f32[32,128]{1,0:T(8,128)S(1)} %bitcast.200, f32[32,128]{1,0:T(8,128)S(1)} %get-tuple-element.266, ...), kind=kOutput, calls=%fused_computation.7.clone.1 | convolution fusion | flops 23605248 | bytes 262656 | tf_op jit(solution)/shard_map/while/body/eval_jaxpr/vmap()/dot_general | solution.py:91
  168.4 3.7 fusion.112
  173.6 5.7 %fusion.111 = f32[16,32,3,128]{3,2,1,0:T(4,128)} fusion(f32[16,32,3,128]{3,2,1,0:T(4,128)} %get-tuple-element.281, s32[]{:T(128)} %get-tuple-element.280, f32[32,128]{1,0:T(8,128)S(1)} %dynamic-slice_bitcast_fusion.4, f32[32,128]{1,0:T(8,128)S(1)} %bitcast.198, f32[32,128]{1,0:T(8,128)S(1)} %bitcast.200, f32[32,128]{1,0:T(8,128)S(1)} %get-tuple-element.266, ...), kind=kOutput, calls=%fused_computation.7.clone.1 | convolution fusion | flops 23605248 | bytes 262656 | tf_op jit(solution)/shard_map/while/body/eval_jaxpr/vmap()/dot_general | solution.py:91
  182.5 3.7 fusion.112
  187.6 5.7 %fusion.111 = f32[16,32,3,128]{3,2,1,0:T(4,128)} fusion(f32[16,32,3,128]{3,2,1,0:T(4,128)} %get-tuple-element.281, s32[]{:T(128)} %get-tuple-element.280, f32[32,128]{1,0:T(8,128)S(1)} %dynamic-slice_bitcast_fusion.4, f32[32,128]{1,0:T(8,128)S(1)} %bitcast.198, f32[32,128]{1,0:T(8,128)S(1)} %bitcast.200, f32[32,128]{1,0:T(8,128)S(1)} %get-tuple-element.266, ...), kind=kOutput, calls=%fused_computation.7.clone.1 | convolution fusion | flops 23605248 | bytes 262656 | tf_op jit(solution)/shard_map/while/body/eval_jaxpr/vmap()/dot_general | solution.py:91
  196.6 3.7 fusion.112
  201.7 5.7 %fusion.111 = f32[16,32,3,128]{3,2,1,0:T(4,128)} fusion(f32[16,32,3,128]{3,2,1,0:T(4,128)} %get-tuple-element.281, s32[]{:T(128)} %get-tuple-element.280, f32[32,128]{1,0:T(8,128)S(1)} %dynamic-slice_bitcast_fusion.4, f32[32,128]{1,0:T(8,128)S(1)} %bitcast.198, f32[32,128]{1,0:T(8,128)S(1)} %bitcast.200, f32[32,128]{1,0:T(8,128)S(1)} %get-tuple-element.266, ...), kind=kOutput, calls=%fused_computation.7.clone.1 | convolution fusion | flops 23605248 | bytes 262656 | tf_op jit(solution)/shard_map/while/body/eval_jaxpr/vmap()/dot_general | solution.py:91
  210.6 3.7 fusion.112
  215.8 5.7 %fusion.111 = f32[16,32,3,128]{3,2,1,0:T(4,128)} fusion(f32[16,32,3,128]{3,2,1,0:T(4,128)} %get-tuple-element.281, s32[]{:T(128)} %get-tuple-element.280, f32[32,128]{1,0:T(8,128)S(1)} %dynamic-slice_bitcast_fusion.4, f32[32,128]{1,0:T(8,128)S(1)} %bitcast.198, f32[32,128]{1,0:T(8,128)S(1)} %bitcast.200, f32[32,128]{1,0:T(8,128)S(1)} %get-tuple-element.266, ...), kind=kOutput, calls=%fused_computation.7.clone.1 | convolution fusion | flops 23605248 | bytes 262656 | tf_op jit(solution)/shard_map/while/body/eval_jaxpr/vmap()/dot_general | solution.py:91
  224.7 3.7 fusion.112
  229.8 5.7 %fusion.111 = f32[16,32,3,128]{3,2,1,0:T(4,128)} fusion(f32[16,32,3,128]{3,2,1,0:T(4,128)} %get-tuple-element.281, s32[]{:T(128)} %get-tuple-element.280, f32[32,128]{1,0:T(8,128)S(1)} %dynamic-slice_bitcast_fusion.4, f32[32,128]{1,0:T(8,128)S(1)} %bitcast.198, f32[32,128]{1,0:T(8,128)S(1)} %bitcast.200, f32[32,128]{1,0:T(8,128)S(1)} %get-tuple-element.266, ...), kind=kOutput, calls=%fused_computation.7.clone.1 | convolution fusion | flops 23605248 | bytes 262656 | tf_op jit(solution)/shard_map/while/body/eval_jaxpr/vmap()/dot_general | solution.py:91
  238.8 3.7 fusion.112
  243.9 5.7 %fusion.111 = f32[16,32,3,128]{3,2,1,0:T(4,128)} fusion(f32[16,32,3,128]{3,2,1,0:T(4,128)} %get-tuple-element.281, s32[]{:T(128)} %get-tuple-element.280, f32[32,128]{1,0:T(8,128)S(1)} %dynamic-slice_bitcast_fusion.4, f32[32,128]{1,0:T(8,128)S(1)} %bitcast.198, f32[32,128]{1,0:T(8,128)S(1)} %bitcast.200, f32[32,128]{1,0:T(8,128)S(1)} %get-tuple-element.266, ...), kind=kOutput, calls=%fused_computation.7.clone.1 | convolution fusion | flops 23605248 | bytes 262656 | tf_op jit(solution)/shard_map/while/body/eval_jaxpr/vmap()/dot_general | solution.py:91
  252.8 3.7 fusion.112
  258.0 5.7 %fusion.111 = f32[16,32,3,128]{3,2,1,0:T(4,128)} fusion(f32[16,32,3,128]{3,2,1,0:T(4,128)} %get-tuple-element.281, s32[]{:T(128)} %get-tuple-element.280, f32[32,128]{1,0:T(8,128)S(1)} %dynamic-slice_bitcast_fusion.4, f32[32,128]{1,0:T(8,128)S(1)} %bitcast.198, f32[32,128]{1,0:T(8,128)S(1)} %bitcast.200, f32[32,128]{1,0:T(8,128)S(1)} %get-tuple-element.266, ...), kind=kOutput, calls=%fused_computation.7.clone.1 | convolution fusion | flops 23605248 | bytes 262656 | tf_op jit(solution)/shard_map/while/body/eval_jaxpr/vmap()/dot_general | solution.py:91
  266.9 3.7 fusion.112
  272.0 5.7 %fusion.111 = f32[16,32,3,128]{3,2,1,0:T(4,128)} fusion(f32[16,32,3,128]{3,2,1,0:T(4,128)} %get-tuple-element.281, s32[]{:T(128)} %get-tuple-element.280, f32[32,128]{1,0:T(8,128)S(1)} %dynamic-slice_bitcast_fusion.4, f32[32,128]{1,0:T(8,128)S(1)} %bitcast.198, f32[32,128]{1,0:T(8,128)S(1)} %bitcast.200, f32[32,128]{1,0:T(8,128)S(1)} %get-tuple-element.266, ...), kind=kOutput, calls=%fused_computation.7.clone.1 | convolution fusion | flops 23605248 | bytes 262656 | tf_op jit(solution)/shard_map/while/body/eval_jaxpr/vmap()/dot_general | solution.py:91
  281.0 3.7 fusion.112
  286.1 5.7 %fusion.111 = f32[16,32,3,128]{3,2,1,0:T(4,128)} fusion(f32[16,32,3,128]{3,2,1,0:T(4,128)} %get-tuple-element.281, s32[]{:T(128)} %get-tuple-element.280, f32[32,128]{1,0:T(8,128)S(1)} %dynamic-slice_bitcast_fusion.4, f32[32,128]{1,0:T(8,128)S(1)} %bitcast.198, f32[32,128]{1,0:T(8,128)S(1)} %bitcast.200, f32[32,128]{1,0:T(8,128)S(1)} %get-tuple-element.266, ...), kind=kOutput, calls=%fused_computation.7.clone.1 | convolution fusion | flops 23605248 | bytes 262656 | tf_op jit(solution)/shard_map/while/body/eval_jaxpr/vmap()/dot_general | solution.py:91
  295.0 3.7 fusion.112
  300.1 5.7 %fusion.111 = f32[16,32,3,128]{3,2,1,0:T(4,128)} fusion(f32[16,32,3,128]{3,2,1,0:T(4,128)} %get-tuple-element.281, s32[]{:T(128)} %get-tuple-element.280, f32[32,128]{1,0:T(8,128)S(1)} %dynamic-slice_bitcast_fusion.4, f32[32,128]{1,0:T(8,128)S(1)} %bitcast.198, f32[32,128]{1,0:T(8,128)S(1)} %bitcast.200, f32[32,128]{1,0:T(8,128)S(1)} %get-tuple-element.266, ...), kind=kOutput, calls=%fused_computation.7.clone.1 | convolution fusion | flops 23605248 | bytes 262656 | tf_op jit(solution)/shard_map/while/body/eval_jaxpr/vmap()/dot_general | solution.py:91
  309.1 3.7 fusion.112
  314.2 5.7 %fusion.111 = f32[16,32,3,128]{3,2,1,0:T(4,128)} fusion(f32[16,32,3,128]{3,2,1,0:T(4,128)} %get-tuple-element.281, s32[]{:T(128)} %get-tuple-element.280, f32[32,128]{1,0:T(8,128)S(1)} %dynamic-slice_bitcast_fusion.4, f32[32,128]{1,0:T(8,128)S(1)} %bitcast.198, f32[32,128]{1,0:T(8,128)S(1)} %bitcast.200, f32[32,128]{1,0:T(8,128)S(1)} %get-tuple-element.266, ...), kind=kOutput, calls=%fused_computation.7.clone.1 | convolution fusion | flops 23605248 | bytes 262656 | tf_op jit(solution)/shard_map/while/body/eval_jaxpr/vmap()/dot_general | solution.py:91
  323.2 3.7 fusion.112
  328.3 5.7 %fusion.111 = f32[16,32,3,128]{3,2,1,0:T(4,128)} fusion(f32[16,32,3,128]{3,2,1,0:T(4,128)} %get-tuple-element.281, s32[]{:T(128)} %get-tuple-element.280, f32[32,128]{1,0:T(8,128)S(1)} %dynamic-slice_bitcast_fusion.4, f32[32,128]{1,0:T(8,128)S(1)} %bitcast.198, f32[32,128]{1,0:T(8,128)S(1)} %bitcast.200, f32[32,128]{1,0:T(8,128)S(1)} %get-tuple-element.266, ...), kind=kOutput, calls=%fused_computation.7.clone.1 | convolution fusion | flops 23605248 | bytes 262656 | tf_op jit(solution)/shard_map/while/body/eval_jaxpr/vmap()/dot_general | solution.py:91
  342.4 5.7 %fusion.111 = f32[16,32,3,128]{3,2,1,0:T(4,128)} fusion(f32[16,32,3,128]{3,2,1,0:T(4,128)} %get-tuple-element.281, s32[]{:T(128)} %get-tuple-element.280, f32[32,128]{1,0:T(8,128)S(1)} %dynamic-slice_bitcast_fusion.4, f32[32,128]{1,0:T(8,128)S(1)} %bitcast.198, f32[32,128]{1,0:T(8,128)S(1)} %bitcast.200, f32[32,128]{1,0:T(8,128)S(1)} %get-tuple-element.266, ...), kind=kOutput, calls=%fused_computation.7.clone.1 | convolution fusion | flops 23605248 | bytes 262656 | tf_op jit(solution)/shard_map/while/body/eval_jaxpr/vmap()/dot_general | solution.py:91
  351.3 3.7 fusion.112
  356.4 5.7 %fusion.111 = f32[16,32,3,128]{3,2,1,0:T(4,128)} fusion(f32[16,32,3,128]{3,2,1,0:T(4,128)} %get-tuple-element.281, s32[]{:T(128)} %get-tuple-element.280, f32[32,128]{1,0:T(8,128)S(1)} %dynamic-slice_bitcast_fusion.4, f32[32,128]{1,0:T(8,128)S(1)} %bitcast.198, f32[32,128]{1,0:T(8,128)S(1)} %bitcast.200, f32[32,128]{1,0:T(8,128)S(1)} %get-tuple-element.266, ...), kind=kOutput, calls=%fused_computation.7.clone.1 | convolution fusion | flops 23605248 | bytes 262656 | tf_op jit(solution)/shard_map/while/body/eval_jaxpr/vmap()/dot_general | solution.py:91
  364.3 13.2 %all-to-all-start.2 = ((f32[64,8,3,128]{3,1,2,0:T(8,128)}), f32[64,8,3,128]{3,1,2,0:T(8,128)}, u32[]{:S(2)}, u32[]{:S(2)}) async-start(f32[64,8,3,128]{3,1,2,0:T(8,128)} %copy.135), calls=%async_computation.2 | async-start | bytes 1572864 | tf_op jit(solution)/shard_map/all_to_all | solution.py:203
  377.5 6.0 %add_multiply_fusion.23 = (f32[1,17,17,129]{3,2,1,0:T(8,128)S(1)}, f32[1,17,17,129]{3,2,1,0:T(8,128)S(1)}, f32[1,17,17,129]{3,2,1,0:T(8,128)S(1)}, f32[1,17,17,1...) fusion(f32[5,18,18,128]{3,2,1,0:T(8,128)S(1)} %copy.115, ...), kind=kLoop, calls=%fused_computation.171 | loop fusion | flops 7903572 | bytes 3527050 | tf_op jit(solution)/shard_map/mul | solution.py:74
  385.6 8.5 %copy.118 = f32[3,16,16,128]{0,3,2,1:T(8,128)} copy(f32[3,16,16,128]{3,2,1,0:T(8,128)S(1)} %fusion.68) | data formatting | bytes 786432 | tf_op jit(solution)/shard_map/add | solution.py:139
  398.8 51.3 %scatter_fusion = f32[3,32768]{0,1:T(8,128)} fusion(f32[3,32768]{0,1:T(8,128)} %bitcast.174, s32[8192]{0:T(1024)S(1)} %bitcast.206, f32[8192,3]{1,0:T(8,128)} %bitcast.179), kind=kCustom, calls=%fused_computation.1 | custom fusion | flops 24576 | bytes 327680 | tf_op jit(solution)/shard_map/scatter-add | solution.py:211
  450.2 10.6 %copy.137 = f32[3,16,16,128]{3,2,1,0:T(8,128)} copy(f32[3,16,16,128]{0,3,2,1:T(8,128)} %bitcast.175) | data formatting | bytes 786432
  (242 shorter events, 126.8 us)
Async XLA Ops:
  0.6 26.3 %copy-start.5 = (s32[64,128]{1,0:T(8,128)S(1)}, s32[64,128]{1,0:T(8,128)}, u32[]{:S(2)}) copy-start(s32[64,128]{1,0:T(8,128)} %param.21) | copy-start | bytes 98308
  0.6 26.2 %copy-start.4 = (f32[256,128]{1,0:T(8,128)S(1)}, f32[256,128]{1,0:T(8,128)}, u32[]{:S(2)}) copy-start(f32[256,128]{1,0:T(8,128)} %param.17) | copy-start | bytes 393220
  1.5 84.2 %collective-permute-start = (f32[5,1,16,128]{3,2,1,0:T(8,128)S(1)}, f32[5,1,16,128]{3,2,1,0:T(8,128)S(1)}, u32[]{:S(2)}, u32[]{:S(2)}) collective-permute-start(f32[5,1,16,128]{3,2,1,0:T(8,128)S(1)} %get-tuple-element.186), channel_id=1, source_target_pairs={{0,64},{64,128},{128,192},{1,65},{65,129},{129,193},{2,66},{66,130... | collective-permute-start | bytes 122888 | tf_op jit(solution)/shard_map/ppermute | solution.py:27
  5.5 80.1 %collective-permute-start.1 = (f32[5,1,16,128]{3,2,1,0:T(8,128)S(1)}, f32[5,1,16,128]{3,2,1,0:T(8,128)S(1)}, u32[]{:S(2)}, u32[]{:S(2)}) collective-permute-start(f32[5,1,16,128]{3,2,1,0:T(8,128)S(1)} %get-tuple-element.187), channel_id=1, source_target_pairs={{64,0},{128,64},{192,128},{65,1},{129,65},{193,129},{66,2},{130,66... | collective-permute-start | bytes 122888 | tf_op jit(solution)/shard_map/ppermute | solution.py:29
  11.4 21.6 %all-to-all-start = ((s32[64,1,8]{2,1,0:T(1,128)}), s32[64,1,8]{2,1,0:T(1,128)S(1)}, u32[]{:S(2)}, u32[]{:S(2)}) async-start(s32[64,1,8]{2,1,0:T(1,128)} %bitcast.28), calls=%async_computation | async-start | bytes 65536 | tf_op jit(solution)/shard_map/all_to_all | solution.py:169
  26.8 12.4 %copy-start.7 = (s32[64,128]{1,0:T(8,128)S(1)}, s32[64,128]{1,0:T(8,128)}, u32[]{:S(2)}) copy-start(s32[64,128]{1,0:T(8,128)} %param.23) | copy-start | bytes 98308
  26.8 12.4 %copy-start.1 = (f32[3,16,16,128]{3,2,1,0:T(8,128)S(1)}, f32[3,16,16,128]{3,2,1,0:T(8,128)}, u32[]{:S(2)}) copy-start(f32[3,16,16,128]{3,2,1,0:T(8,128)} %param.13) | copy-start | bytes 1179652
  33.0 101.1 %all-to-all-start.1 = ((f32[64,8,4,128]{3,1,2,0:T(8,128)}), f32[64,8,4,128]{3,1,2,0:T(8,128)}, u32[]{:S(2)}, u32[]{:S(2)}) async-start(f32[64,8,4,128]{3,1,2,0:T(8,128)} %fusion.29), calls=%async_computation.1 | async-start | bytes 2097152 | tf_op jit(solution)/shard_map/all_to_all | solution.py:168
  81.4 4.3 copy-start.2
  81.4 4.3 copy-start.3
  81.4 9.9 %copy-start.6 = (f32[64,3,128]{2,0,1:T(8,128)S(1)}, f32[64,3,128]{2,0,1:T(8,128)}, u32[]{:S(2)}) copy-start(f32[64,3,128]{2,0,1:T(8,128)} %param.22) | copy-start | bytes 294916
  85.9 11.5 %collective-permute-start.2 = (f32[5,18,1,128]{3,1,2,0:T(8,128)S(1)}, f32[5,18,1,128]{3,1,2,0:T(8,128)S(1)}, u32[]{:S(2)}, u32[]{:S(2)}) collective-permute-start(f32[5,18,1,128]{3,1,2,0:T(8,128)S(1)} %copy.147), channel_id=1, source_target_pairs={{0,8},{8,16},{16,24},{24,32},{32,40},{40,48},{48,56},{1,9},{9,17},... | collective-permute-start | bytes 138248 | tf_op jit(solution)/shard_map/ppermute | solution.py:27
  89.4 12.7 %collective-permute-start.3 = (f32[5,18,1,128]{3,1,2,0:T(8,128)S(1)}, f32[5,18,1,128]{3,1,2,0:T(8,128)S(1)}, u32[]{:S(2)}, u32[]{:S(2)}) collective-permute-start(f32[5,18,1,128]{3,1,2,0:T(8,128)S(1)} %copy.148), channel_id=1, source_target_pairs={{8,0},{16,8},{24,16},{32,24},{40,32},{48,40},{56,48},{9,1},{17,9},... | collective-permute-start | bytes 138248 | tf_op jit(solution)/shard_map/ppermute | solution.py:29
  116.8 3.1 copy-start
  119.9 11.8 %collective-permute-start.4 = (f32[5,18,18,1]{2,1,3,0:T(8,128)S(1)}, f32[5,18,18,1]{2,1,3,0:T(8,128)S(1)}, u32[]{:S(2)}, u32[]{:S(2)}) collective-permute-start(f32[5,18,18,1]{2,1,3,0:T(8,128)S(1)} %get-tuple-element.155), channel_id=1, source_target_pairs={{0,1},{1,2},{2,3},{3,4},{4,5},{5,6},{6,7},{8,9},{9,10},{10,11},{11... | collective-permute-start | bytes 19448 | tf_op jit(solution)/shard_map/ppermute | solution.py:27
  123.0 9.4 %collective-permute-start.5 = (f32[5,18,18,1]{2,1,3,0:T(8,128)S(1)}, f32[5,18,18,1]{2,1,3,0:T(8,128)S(1)}, u32[]{:S(2)}, u32[]{:S(2)}) collective-permute-start(f32[5,18,18,1]{2,1,3,0:T(8,128)S(1)} %get-tuple-element.154), channel_id=1, source_target_pairs={{1,0},{2,1},{3,2},{4,3},{5,4},{6,5},{7,6},{9,8},{10,9},{11,10},{12... | collective-permute-start | bytes 19448 | tf_op jit(solution)/shard_map/ppermute | solution.py:29
  364.3 96.5 %all-to-all-start.2 = ((f32[64,8,3,128]{3,1,2,0:T(8,128)}), f32[64,8,3,128]{3,1,2,0:T(8,128)}, u32[]{:S(2)}, u32[]{:S(2)}) async-start(f32[64,8,3,128]{3,1,2,0:T(8,128)} %copy.135), calls=%async_computation.2 | async-start | bytes 1572864 | tf_op jit(solution)/shard_map/all_to_all | solution.py:203
where the time goes:
time: 470 us; the launch traced here: 464 us
  local copies, waits for them, and re-layouts  167 us (36%)
  matrix products  155 us (33%)
  other arithmetic  88.6 us (19%)
  starting transfers between devices  47.2 us (10%)
    dot_general x16, matrix products, contact_block(): jnp.dot(areas, intersection.T, precision=lax.Precision.HIGHEST)  91.1 us
    dot_general x16, matrix products, contact_block(): jnp.dot(stiffness, intersection, precision=lax.Precision.HIGHEST)[None, :]  59.5 us
    scatter-add x1, other arithmetic, body(): node_force.reshape(3, -1).at[:, master_node.reshape(-1)].add(reaction_flat)  51.3 us
    gather x2, local copies, waits for them, and re-layouts, body(): centers = jnp.transpose(flat_moves[:, master_node], (1, 0, 2))  36.5 us
    dynamic_slice x64, local copies, waits for them, and re-layouts, body(): lax.map(per_group, (arrived[:, 0:3].reshape(groups, 32, 3, block_width),...  25.9 us
    unnamed x24, local copies, waits for them, and re-layouts  25.8 us
    all_to_all x1, starting transfers between devices, body(): lax.all_to_all(pushes, ('gy', 'gz'), split_axis=0, concat_axis=0, tiled=T...  13.2 us
    squeeze x16, local copies, waits for them, and re-layouts, body(): lax.map(per_group, (arrived[:, 0:3].reshape(groups, 32, 3, block_width),...  13 us
  transfers between devices with their start and end apart: 9, of which 1 were waited for; matrix products, arithmetic and copies ran while one was open for 37% of the time, Pallas kernels for 0%

commit v1 on v0

v1 whole, which is shorter than its diff:
```python
import functools

import jax
import jax.numpy as jnp
from jax import lax
from jax.experimental import pallas as pl
from jax.experimental.pallas import tpu as pltpu
from jax.sharding import PartitionSpec as P

f32 = jnp.float32
bf16 = jnp.bfloat16
i32 = jnp.int32
NT = (((1,), (1,)), ((), ()))
MESH = pl.DeviceIdType.MESH
VMEM = pl.BlockSpec(memory_space=pltpu.VMEM)
SLOTS = 8
LANES = 128

gamma_gas = 5.0 / 3.0
corner_offsets = [
    (0, 0, 0),
    (0, 0, 1),
    (0, 1, 0),
    (0, 1, 1),
    (1, 0, 0),
    (1, 0, 1),
    (1, 1, 0),
    (1, 1, 1),
]


def split3(x):
    first = x.astype(bf16)
    rest = x - first.astype(f32)
    second = rest.astype(bf16)
    third = (rest - second.astype(f32)).astype(bf16)
    return first, second, third


def dot(left, right):
    return jnp.dot(left, right, preferred_element_type=f32)


def iota(shape, axis):
    return lax.broadcasted_iota(i32, shape, axis)


def gather_centers(disp, mnode, centers, table):
    rows = disp.shape[1] * disp.shape[2]
    for c in range(3):
        turned = jnp.transpose(disp[c].reshape(rows, LANES))
        for s, part in enumerate(split3(turned)):
            table[c * LANES : (c + 1) * LANES, s * rows : (s + 1) * rows] = part
    row_at = iota((rows, 2 * LANES), 0)
    lane_at = iota((LANES, 2 * LANES), 0)

    def step(q, carry):
        index = jnp.concatenate([mnode[pl.ds(2 * q + u, 1), :] for u in range(2)], axis=1)
        hot = (lax.shift_right_logical(index, 7) == row_at).astype(f32).astype(bf16)
        picked = dot(table[...], jnp.concatenate([hot, hot, hot], axis=0))
        here = (index & (LANES - 1)) == lane_at
        for c in range(3):
            row = jnp.sum(
                jnp.where(here, picked[c * LANES : (c + 1) * LANES], 0.0), axis=0, keepdims=True
            )
            for u in range(2):
                centers[c, pl.ds(2 * q + u, 1), :] = row[:, u * LANES : (u + 1) * LANES]
        return carry

    lax.fori_loop(0, mnode.shape[0] // 2, step, 0, unroll=4)


def contact_slots(master, slave):
    m1, m2, m3 = [part.astype(f32) for part in split3(master)]
    s1, s2, s3 = [part.astype(f32) for part in split3(slave)]
    zero = jnp.zeros_like(master)
    turned = jnp.concatenate(
        [
            jnp.transpose(jnp.concatenate([m1, m2, m3, m1], axis=0)),
            jnp.transpose(jnp.concatenate([m2, m1, zero, zero], axis=0)),
        ],
        axis=1,
    ).astype(bf16)
    weights = jnp.concatenate([s1, s1, s1, s2, s2, s3, zero, zero], axis=0)
    slot_row = iota((256, LANES), 0) & (SLOTS - 1)
    areas = jnp.concatenate([m1[:24], zero[:8], m2[:24], zero[:8]], axis=0).astype(bf16)
    areas = jnp.concatenate([areas, areas], axis=1)
    push_row = iota((64, LANES), 0) & (SLOTS - 1)
    push = jnp.zeros((64, LANES), f32)
    columns = []
    for q in range(SLOTS // 2):
        chosen = jnp.concatenate(
            [jnp.where(slot_row == 2 * q + u, weights, 0.0).astype(bf16) for u in range(2)], axis=1
        )
        depth = jnp.maximum(dot(turned, chosen), 0.0)
        high = depth.astype(bf16)
        low = (depth - high.astype(f32)).astype(bf16)
        sums = dot(areas, jnp.concatenate([high, low], axis=0))
        for u in range(2):
            half = slice(u * LANES, (u + 1) * LANES)
            push = jnp.where(push_row == 2 * q + u, sums[:, half], push)
            columns.append(jnp.sum(depth[:, half], axis=1, keepdims=True))
    return push[:24] + push[32:56], jnp.transpose(jnp.concatenate(columns, axis=1))


def exchange_kernel(
    size_y,
    size_z,
    disp,
    spos,
    sstiff,
    sactive,
    peer,
    block,
    mnode,
    marea,
    factive,
    push_out,
    total_out,
    place_out,
    ask_send,
    ask_recv,
    give_send,
    give_recv,
    back_send,
    back_recv,
    slave,
    centers,
    table,
    hot_t,
    ask_sems,
    give_sems,
    back_sems,
):
    peers = size_y * size_z
    count = peer.shape[1]
    masters = mnode.shape[0]
    gx, gy, gz = lax.axis_index("gx"), lax.axis_index("gy"), lax.axis_index("gz")

    def device_ahead(t):
        return (gx, lax.rem(gy + t // size_z, size_y), lax.rem(gz + t % size_z, size_z))

    def device_behind(t):
        return (
            gx,
            lax.rem(gy + size_y - t // size_z, size_y),
            lax.rem(gz + size_z - t % size_z, size_z),
        )

    barrier = pltpu.get_barrier_semaphore()

    def greet(t, carry):
        pl.semaphore_signal(barrier, inc=1, device_id=device_ahead(t), device_id_type=MESH)
        return carry

    lax.fori_loop(1, peers, greet, 0)

    named = peer[...]
    ahead = lax.rem(named // size_z - gy + size_y, size_y) * size_z + lax.rem(
        named % size_z - gz + size_z, size_z
    )
    to_peer = (ahead == iota((peers, count), 0)).astype(f32)
    before = (iota((count, count), 0) < iota((count, count), 1)).astype(f32).astype(bf16)
    rank = jnp.sum(to_peer * dot(to_peer.astype(bf16), before), axis=0, keepdims=True).astype(i32)
    place = ahead * SLOTS + rank
    place_out[...] = jnp.broadcast_to(place, place_out.shape)
    in_rank = jnp.where(rank == iota((LANES, count), 0), (block[...] + 1).astype(f32), 0.0)
    asked = lax.dot_general(
        to_peer.astype(bf16), in_rank.astype(bf16), NT, preferred_element_type=f32
    )
    for t in range(peers):
        ask_send[t] = asked[t : t + 1, :]
    ask_recv[0] = asked[0:1, :]

    pl.semaphore_wait(barrier, peers - 1)

    def ask_copy(t):
        return pltpu.make_async_remote_copy(
            src_ref=ask_send.at[t],
            dst_ref=ask_recv.at[t],
            send_sem=ask_sems.at[0, t],
            recv_sem=ask_sems.at[1, t],
            device_id=device_ahead(t),
            device_id_type=MESH,
        )

    def give_copy(t):
        return pltpu.make_async_remote_copy(
            src_ref=give_send.at[t],
            dst_ref=give_recv.at[t],
            send_sem=give_sems.at[0, t],
            recv_sem=give_sems.at[1, t],
            device_id=device_behind(t),
            device_id_type=MESH,
        )

    def back_copy(t):
        return pltpu.make_async_remote_copy(
            src_ref=back_send.at[t],
            dst_ref=back_recv.at[t],
            send_sem=back_sems.at[0, t],
            recv_sem=back_sems.at[1, t],
            device_id=device_ahead(t),
            device_id_type=MESH,
        )

    def ask_start(t, carry):
        ask_copy(t).start()
        return carry

    lax.fori_loop(1, peers, ask_start, 0)

    gather_centers(disp, mnode, centers, table)
    live = factive[...].astype(f32)
    areas = [marea[c] * live for c in range(3)]
    moved = areas[0] * centers[0] + areas[1] * centers[1] + areas[2] * centers[2]
    pack = jnp.concatenate(areas + [moved], axis=1)
    pack3 = jnp.concatenate(split3(pack), axis=0)

    def ask_wait(t, carry):
        ask_copy(t).wait_recv()
        return carry

    lax.fori_loop(1, peers, ask_wait, 0)
    diagonal = (iota((peers, SLOTS, LANES), 1) == iota((peers, SLOTS, LANES), 2)).astype(f32)
    wanted = jnp.sum(
        jnp.broadcast_to(ask_recv[...], (peers, SLOTS, LANES)) * diagonal, axis=2, keepdims=True
    )
    wanted = wanted.astype(i32).reshape(peers * SLOTS, 1) - 1
    hot = (wanted == iota((peers * SLOTS, masters), 1)).astype(f32)
    hot_t[...] = jnp.transpose(
        (wanted == iota((peers * SLOTS, LANES), 1)).astype(f32)
    ).astype(bf16)
    hot3 = jnp.concatenate([hot, hot, hot], axis=1).astype(bf16)
    given = dot(hot3, pack3)
    for c in range(4):
        give_send[:, c * SLOTS : (c + 1) * SLOTS, :] = given[
            :, c * LANES : (c + 1) * LANES
        ].reshape(peers, SLOTS, LANES)

    def give_start(t, carry):
        give_copy(t).start()
        return carry

    lax.fori_loop(1, peers, give_start, 0)
    give_recv[0] = give_send[0]

    stiff = sstiff[...] * sactive[...].astype(f32)
    slots = (place == iota((peers * SLOTS, count), 0)).astype(f32).astype(bf16)
    for c in range(4):
        field = stiff if c == 3 else -(stiff * spos[c])
        parts = split3(field)
        rows = dot(slots, parts[0]) + dot(slots, parts[1]) + dot(slots, parts[2])
        slave[:, c * SLOTS : (c + 1) * SLOTS, :] = rows.reshape(peers, SLOTS, LANES)

    step_of = 4

    def contact(q, carry):
        for u in range(step_of):
            t = q * step_of + u

            @pl.when(t > 0)
            def _():
                give_copy(t).wait_recv()

        for u in range(step_of):
            t = q * step_of + u
            push, total = contact_slots(give_recv[t], slave[t])
            push_out[t] = push
            back_send[t] = total
        for u in range(step_of):
            t = q * step_of + u

            @pl.when(t > 0)
            def _():
                back_copy(t).start()

        return carry

    lax.fori_loop(0, peers // step_of, contact, 0)
    back_recv[0] = back_send[0]

    def finish(t, carry):
        back_copy(t).wait_recv()
        back_copy(t).wait_send()
        give_copy(t).wait_send()
        ask_copy(t).wait_send()
        return carry

    lax.fori_loop(1, peers, finish, 0)
    parts = split3(back_recv[...].reshape(peers * SLOTS, LANES))
    turned = hot_t[0:masters, :]
    total_out[...] = dot(turned, parts[0]) + dot(turned, parts[1]) + dot(turned, parts[2])


def scatter_kernel(push, total, place, mnode, marea, zone, node_out, slave_out, grid):
    masters = mnode.shape[0]
    peers = push.shape[0]
    count = place.shape[1]
    rows = zone.shape[1]

    turned = jnp.transpose(place[...])
    slots = (turned[:, 0:1] == iota((count, peers * SLOTS), 1)).astype(f32).astype(bf16)
    for c in range(3):
        field = push[:, c * SLOTS : (c + 1) * SLOTS, :].reshape(peers * SLOTS, LANES)
        parts = split3(field)
        slave_out[c] = dot(slots, parts[0]) + dot(slots, parts[1]) + dot(slots, parts[2])

    row_at = iota((rows, 2 * LANES), 0)
    lane_at = iota((LANES, 2 * LANES), 0)
    grid[...] = jnp.zeros_like(grid)

    def step(q, carry):
        pair = [pl.ds(2 * q + u, 1) for u in range(2)]
        index = jnp.concatenate([mnode[at, :] for at in pair], axis=1)
        hot = (lax.shift_right_logical(index, 7) == row_at).astype(f32).astype(bf16)
        here = (index & (LANES - 1)) == lane_at
        high, low = [], []
        for c in range(3):
            force = -jnp.concatenate([marea[c, at, :] * total[at, :] for at in pair], axis=1)
            first = force.astype(bf16).astype(f32)
            high.append(jnp.where(here, first, 0.0).astype(bf16))
            low.append(jnp.where(here, force - first, 0.0).astype(bf16))
        spread = jnp.concatenate(
            [jnp.concatenate(high, axis=0), jnp.concatenate(low, axis=0)], axis=1
        )
        grid[...] += lax.dot_general(
            spread, jnp.concatenate([hot, hot], axis=1), NT, preferred_element_type=f32
        )
        return carry

    lax.fori_loop(0, masters // 2, step, 0, unroll=4)
    for c in range(3):
        node_out[c] = zone[c] + jnp.transpose(grid[c * LANES : (c + 1) * LANES, :])


def extended_2(cells, sides, width):
    for axis, dim in sides:
        count = lax.axis_size(axis)
        ends = count - 1
        head = lax.slice_in_dim(cells, 0, width, axis=dim)
        tail = lax.slice_in_dim(cells, cells.shape[dim] - width, cells.shape[dim], axis=dim)
        cells = jnp.concatenate(
            [
                lax.ppermute(tail, axis, [(i, (i + 1) % count) for i in range(ends)]),
                cells,
                lax.ppermute(head, axis, [((i + 1) % count, i) for i in range(ends)]),
            ],
            axis=dim,
        )
    return cells


def cross_parts(left, right):
    return [
        left[1] * right[2] - left[2] * right[1],
        left[2] * right[0] - left[0] * right[2],
        left[0] * right[1] - left[1] * right[0],
    ]


def zone_state(corner_moves, masses, energies, valid):
    edges = []
    for axis_pick in range(3):
        parts = []
        for comp in range(3):
            total = jnp.zeros_like(masses)
            for moved, offset in zip(corner_moves, corner_offsets):
                total = total + (2.0 * offset[axis_pick] - 1.0) * moved[comp]
            total = total * 0.25
            if comp == axis_pick:
                total = total + 1.0
            parts.append(total)
        edges.append(parts)
    cross_yz = cross_parts(edges[1], edges[2])
    cross_zx = cross_parts(edges[2], edges[0])
    cross_xy = cross_parts(edges[0], edges[1])
    volume = edges[0][0] * cross_yz[0] + edges[0][1] * cross_yz[1] + edges[0][2] * cross_yz[2]
    pressure = jnp.where(
        valid, (gamma_gas - 1.0) * masses * energies / jnp.where(valid, volume, 1.0), 0.0
    )
    return (pressure, cross_yz, cross_zx, cross_xy)


def corner_force(state, offset):
    pressure, cross_yz, cross_zx, cross_xy = state
    sign_x = 2.0 * offset[0] - 1.0
    sign_y = 2.0 * offset[1] - 1.0
    sign_z = 2.0 * offset[2] - 1.0
    return jnp.stack(
        [
            pressure
            * 0.25
            * (sign_x * cross_yz[comp] + sign_y * cross_zx[comp] + sign_z * cross_xy[comp])
            for comp in range(3)
        ]
    )


def axis_valid(position, count, length):
    global_row = position * count + jnp.arange(count + 1, dtype=jnp.int32) - 1
    return (global_row >= 0) & (global_row <= length - 2)


def zone_part(displacement, zone_mass, zone_energy):
    cells_x, cells_y, cells_z = (
        displacement.shape[1],
        displacement.shape[2],
        displacement.shape[3],
    )
    fields = jnp.concatenate([displacement, zone_mass[None], zone_energy[None]], axis=0)
    extended = extended_2(fields, (("gx", 1), ("gy", 2), ("gz", 3)), 1)
    valid_x = axis_valid(lax.axis_index("gx"), cells_x, cells_x * lax.axis_size("gx"))
    valid_y = axis_valid(lax.axis_index("gy"), cells_y, cells_y * lax.axis_size("gy"))
    valid_z = axis_valid(lax.axis_index("gz"), cells_z, cells_z * lax.axis_size("gz"))
    valid = valid_x[:, None, None] & valid_y[None, :, None] & valid_z[None, None, :]
    corner_moves = [
        extended[0:3, a : a + cells_x + 1, b : b + cells_y + 1, e : e + cells_z + 1]
        for a, b, e in corner_offsets
    ]
    masses = extended[3, : cells_x + 1, : cells_y + 1, : cells_z + 1]
    energies = extended[4, : cells_x + 1, : cells_y + 1, : cells_z + 1]
    state = zone_state(corner_moves, masses, energies, valid)
    node_force = jnp.zeros((3, cells_x, cells_y, cells_z), jnp.float32)
    for offset in corner_offsets:
        a, b, e = offset
        forces = corner_force(state, offset)
        node_force = (
            node_force
            + forces[:, 1 - a : 1 - a + cells_x, 1 - b : 1 - b + cells_y, 1 - e : 1 - e + cells_z]
        )
    return node_force


def body(
    displacement,
    zone_mass,
    zone_energy,
    slave_position,
    slave_stiffness,
    slave_active,
    partner_peer,
    partner_block,
    master_node,
    master_area,
    face_active,
):
    size_y = lax.axis_size("gy")
    size_z = lax.axis_size("gz")
    peers = size_y * size_z
    count = slave_position.shape[0]
    masters = master_node.shape[0]
    cells = displacement.shape[1:]
    rows = cells[0] * cells[1]
    area = jnp.transpose(master_area, (1, 0, 2))
    push, total, place = pl.pallas_call(
        functools.partial(exchange_kernel, size_y, size_z),
        out_shape=(
            jax.ShapeDtypeStruct((peers, 24, LANES), f32),
            jax.ShapeDtypeStruct((masters, LANES), f32),
            jax.ShapeDtypeStruct((8, count), i32),
        ),
        in_specs=[VMEM] * 9,
        out_specs=(VMEM,) * 3,
        scratch_shapes=[
            pltpu.VMEM((peers, 1, LANES), f32),
            pltpu.VMEM((peers, 1, LANES), f32),
            pltpu.VMEM((peers, 32, LANES), f32),
            pltpu.VMEM((peers, 32, LANES), f32),
            pltpu.VMEM((peers, 8, LANES), f32),
            pltpu.VMEM((peers, 8, LANES), f32),
            pltpu.VMEM((peers, 32, LANES), f32),
            pltpu.VMEM((3, masters, LANES), f32),
            pltpu.VMEM((3 * LANES, 3 * rows), bf16),
            pltpu.VMEM((LANES, peers * SLOTS), bf16),
            pltpu.SemaphoreType.DMA((2, peers)),
            pltpu.SemaphoreType.DMA((2, peers)),
            pltpu.SemaphoreType.DMA((2, peers)),
        ],
        compiler_params=pltpu.CompilerParams(
            collective_id=0, has_side_effects=True, vmem_limit_bytes=48 * 2**20
        ),
        name="exchange",
    )(
        displacement,
        jnp.transpose(slave_position, (1, 0, 2)),
        slave_stiffness,
        slave_active,
        partner_peer.reshape(1, count),
        partner_block.reshape(1, count),
        master_node,
        area,
        face_active,
    )
    zone = zone_part(displacement, zone_mass, zone_energy)
    node_force, slave_force = pl.pallas_call(
        scatter_kernel,
        out_shape=(
            jax.ShapeDtypeStruct((3, rows, LANES), f32),
            jax.ShapeDtypeStruct((3, count, LANES), f32),
        ),
        in_specs=[VMEM] * 6,
        out_specs=(VMEM,) * 2,
        scratch_shapes=[pltpu.VMEM((3 * LANES, rows), f32)],
        compiler_params=pltpu.CompilerParams(vmem_limit_bytes=48 * 2**20),
        name="scatter",
    )(push, total, place, master_node, area, zone.reshape(3, rows, LANES))
    return (
        node_force.reshape((3,) + cells),
        jnp.transpose(slave_force, (1, 0, 2)),
    )


def solution(mesh):
    return jax.shard_map(
        body,
        mesh=mesh,
        in_specs=(
            P(None, "gx", "gy", "gz"),
            P("gx", "gy", "gz"),
            P("gx", "gy", "gz"),
            P(("gx", "gy", "gz"), None, None),
            P(("gx", "gy", "gz"), None),
            P(("gx", "gy", "gz"), None),
            P(("gx", "gy", "gz"), None),
            P(("gx", "gy", "gz"), None),
            P(("gx", "gy", "gz"), None),
            P(("gx", "gy", "gz"), None, None),
            P(("gx", "gy", "gz"), None),
        ),
        out_specs=(P(None, "gx", "gy", "gz"), P(("gx", "gy", "gz"), None, None)),
        check_vma=False,
    )
```

time: 470 us -> 129 us (0.27); the launches traced: 464 us -> 129 us
  matrix products: 155 us -> 0 us
  local copies, waits for them, and re-layouts: 167 us -> 22.2 us
  other arithmetic: 88.6 us -> 20.1 us
  Pallas kernels: 0 us -> 64.5 us
  starting transfers between devices: 47.2 us -> 17.4 us
    dot_general x36 -> x0, matrix products: 155 us -> none  [the longest x16 91.1 us: contact_block(): jnp.dot(areas, intersection.T, precision=lax.Precision.HIGHEST)]
    pallas_call x0 -> x2, Pallas kernels: none -> 64.5 us  [the longest x1 57.5 us: body(): pl.pallas_call(functools.partial(exchange_kernel, size_y, size_z), out_sh...]
    scatter-add x1 -> x0, other arithmetic: 51.3 us -> none  [body(): node_force.reshape(3, -1).at[:, master_node.reshape(-1)].add(reaction_flat)]
    gather x2 -> x0, local copies, waits for them, and re-layouts: 36.5 us -> none  [body(): centers = jnp.transpose(flat_moves[:, master_node], (1, 0, 2))]
    all_to_all x3 -> x0, starting transfers between devices: 31.9 us -> none  [the longest x1 13.2 us: body(): lax.all_to_all(pushes, ('gy', 'gz'), split_axis=0, concat_axis=0, tiled=T...]
    dynamic_slice x64 -> x0, local copies, waits for them, and re-layouts: 25.9 us -> none  [body(): lax.map(per_group, (arrived[:, 0:3].reshape(groups, 32, 3, block_width),...]
    unnamed x24, local copies, waits for them, and re-layouts: 25.8 us -> 0.2 us
    mul x48 -> x0, local copies, waits for them, and re-layouts: 23.1 us -> none  [the longest x16 11.5 us: contact_block(): stiffness[None, :]]
  transfers between devices with their start and end apart: 9 -> 6, of which waited for: 1 -> 1; matrix products, arithmetic and copies ran while one was open for 37% -> 12% of each run, Pallas kernels for 0% -> 45%
where the time goes in v1:
time: 129 us
  Pallas kernels  64.5 us (50%)
  local copies, waits for them, and re-layouts  22.2 us (17%)
  other arithmetic  20.1 us (16%)
  starting transfers between devices  17.4 us (13%)
  waiting for transfers between devices  3.43 us (3%)
    pallas_call x1, Pallas kernels, body(): pl.pallas_call(functools.partial(exchange_kernel, size_y, size_z), out_sh...  57.5 us
    ppermute x3, starting transfers between devices, extended_2(): lax.ppermute(tail, axis, [(i, (i + 1) % count) for i in range(ends)])  12.7 us
    concatenate x3, other arithmetic, extended_2(): jnp.concatenate([lax.ppermute(tail, axis, [(i, (i + 1) % count) for i in...  12.4 us
    concatenate x2, local copies, waits for them, and re-layouts, extended_2(): jnp.concatenate([lax.ppermute(tail, axis, [(i, (i + 1) % count) for i in...  10.1 us
    pallas_call x1, Pallas kernels, body(): pl.pallas_call(scatter_kernel, out_shape=(jax.ShapeDtypeStruct((3, rows,...  6.94 us
    ppermute x2, local copies, waits for them, and re-layouts, extended_2(): lax.ppermute(head, axis, [((i + 1) % count, i) for i in range(ends)])  6.41 us
    mul x3, other arithmetic, corner_force(): pressure * 0.25  6.22 us
    ppermute x2, local copies, waits for them, and re-layouts, extended_2(): lax.ppermute(tail, axis, [(i, (i + 1) % count) for i in range(ends)])  5.49 us
  transfers between devices with their start and end apart: 6, of which 1 were waited for; matrix products, arithmetic and copies ran while one was open for 12% of the time, Pallas kernels for 45%

profile of v1, /device:TPU:1, one launch (start us, length us, event | category | flops | bytes accessed | tf_op | source)
XLA Modules:
  0.0 128.6 jit_solution(16050673804386612033)
XLA Ops:
  0.6 0.8 pad_maximum_fusion.22
  1.5 4.0 %collective-permute-start = (f32[5,1,16,128]{3,2,1,0:T(8,128)S(1)}, f32[5,1,16,128]{3,2,1,0:T(8,128)S(1)}, u32[]{:S(2)}, u32[]{:S(2)}) collective-permute-start(f32[5,1,16,128]{3,2,1,0:T(8,128)S(1)} %get-tuple-element.64), channel_id=1, source_target_pairs={{0,64},{64,128},{128,192},{1,65},{65,129},{129,193},{2,66},{66,130... | collective-permute-start | bytes 122888 | tf_op jit(solution)/shard_map/ppermute | solution.py:345
  5.5 1.3 %collective-permute-start.1 = (f32[5,1,16,128]{3,2,1,0:T(8,128)S(1)}, f32[5,1,16,128]{3,2,1,0:T(8,128)S(1)}, u32[]{:S(2)}, u32[]{:S(2)}) collective-permute-start(f32[5,1,16,128]{3,2,1,0:T(8,128)S(1)} %get-tuple-element.65), channel_id=1, source_target_pairs={{64,0},{128,64},{192,128},{65,1},{129,65},{193,129},{66,2},{130,66... | collective-permute-start | bytes 122888 | tf_op jit(solution)/shard_map/ppermute | solution.py:347
  6.8 0.0 collective-permute-done
  6.8 3.4 %collective-permute-done.1 = f32[5,1,16,128]{3,2,1,0:T(8,128)S(1)} collective-permute-done((f32[5,1,16,128]{3,2,1,0:T(8,128)S(1)}, f32[5,1,16,128]{3,2,1,0:T(8,128)S(1)}, u32[]{:S(2)}, u32[]{:S(2)}) %collective-permute-start.1) | collective-permute-done | bytes 40992 | tf_op jit(solution)/shard_map/ppermute | solution.py:347
  10.2 1.2 pad_maximum_fusion.1
  11.4 0.1 fusion.40
  11.5 5.1 %collective-permute-start.2 = (f32[5,18,1,128]{3,1,2,0:T(8,128)S(1)}, f32[5,18,1,128]{3,1,2,0:T(8,128)S(1)}, u32[]{:S(2)}, u32[]{:S(2)}) collective-permute-start(f32[5,18,1,128]{3,1,2,0:T(8,128)S(1)} %copy.34), channel_id=1, source_target_pairs={{0,8},{8,16},{16,24},{24,32},{32,40},{40,48},{48,56},{1,9},{9,17},... | collective-permute-start | bytes 138248 | tf_op jit(solution)/shard_map/ppermute | solution.py:345
  16.7 1.9 %collective-permute-start.3 = (f32[5,18,1,128]{3,1,2,0:T(8,128)S(1)}, f32[5,18,1,128]{3,1,2,0:T(8,128)S(1)}, u32[]{:S(2)}, u32[]{:S(2)}) collective-permute-start(f32[5,18,1,128]{3,1,2,0:T(8,128)S(1)} %copy.35), channel_id=1, source_target_pairs={{8,0},{16,8},{24,16},{32,24},{40,32},{48,40},{56,48},{9,1},{17,9},... | collective-permute-start | bytes 138248 | tf_op jit(solution)/shard_map/ppermute | solution.py:347
  18.6 0.1 broadcast_and_fusion
  18.7 4.9 %copy.28 = f32[5,18,16,128]{2,1,3,0:T(8,128)} copy(f32[5,18,16,128]{3,2,1,0:T(8,128)S(1)} %pad_maximum_fusion.1) | data formatting | bytes 1474560 | tf_op jit(solution)/shard_map/concatenate | solution.py:343
  23.5 0.0 collective-permute-done.2
  23.5 4.8 %copy.27 = f32[5,18,1,128]{2,1,3,0:T(8,128)} copy(f32[5,18,1,128]{3,1,2,0:T(8,128)S(1)} %collective-permute-done.2) | data formatting | bytes 92160 | tf_op jit(solution)/shard_map/ppermute | solution.py:345
  28.4 0.0 collective-permute-done.3
  28.4 4.7 %copy.29 = f32[5,18,1,128]{2,1,3,0:T(8,128)} copy(f32[5,18,1,128]{3,1,2,0:T(8,128)S(1)} %collective-permute-done.3) | data formatting | bytes 92160 | tf_op jit(solution)/shard_map/ppermute | solution.py:347
  33.1 0.0 copy-start
  33.1 0.0 copy-start.4
  33.1 0.0 copy-start.5
  33.2 0.0 copy-start.6
  33.2 0.0 copy-start.7
  33.2 0.0 copy-start.8
  33.2 10.0 %pad_maximum_fusion = f32[5,18,18,128]{2,1,3,0:T(8,128)S(1)} fusion(f32[5,18,1,128]{2,1,3,0:T(8,128)} %copy.29, f32[5,18,16,128]{2,1,3,0:T(8,128)} %copy.28, f32[5,18,1,128]{2,1,3,0:T(8,128)} %copy.27), kind=kLoop, calls=%fused_computation | loop fusion | flops 414720 | bytes 1658880 | tf_op jit(solution)/shard_map/concatenate | solution.py:343
  43.2 0.0 copy-start.9
  43.2 3.5 %collective-permute-start.4 = (f32[5,18,18,1]{2,1,3,0:T(8,128)S(1)}, f32[5,18,18,1]{2,1,3,0:T(8,128)S(1)}, u32[]{:S(2)}, u32[]{:S(2)}) collective-permute-start(f32[5,18,18,1]{2,1,3,0:T(8,128)S(1)} %get-tuple-element.35), channel_id=1, source_target_pairs={{0,1},{1,2},{2,3},{3,4},{4,5},{5,6},{6,7},{8,9},{9,10},{10,11},{11... | collective-permute-start | bytes 19448 | tf_op jit(solution)/shard_map/ppermute | solution.py:345
  46.8 1.5 %collective-permute-start.5 = (f32[5,18,18,1]{2,1,3,0:T(8,128)S(1)}, f32[5,18,18,1]{2,1,3,0:T(8,128)S(1)}, u32[]{:S(2)}, u32[]{:S(2)}) collective-permute-start(f32[5,18,18,1]{2,1,3,0:T(8,128)S(1)} %get-tuple-element.34), channel_id=1, source_target_pairs={{1,0},{2,1},{3,2},{4,3},{5,4},{6,5},{7,6},{9,8},{10,9},{11,10},{12... | collective-permute-start | bytes 19448 | tf_op jit(solution)/shard_map/ppermute | solution.py:347
  48.3 0.0 copy-done.9
  48.3 0.0 copy-done
  48.3 0.0 copy-done.1
  48.3 0.0 copy-done.2
  48.3 0.0 copy-done.3
  48.3 0.0 copy-done.4
  48.3 0.0 copy-done.5
  48.3 0.0 copy-done.6
  48.3 0.0 copy-done.7
  48.3 0.0 copy-done.8
  48.4 57.5 %exchange.1 = (f32[64,24,128]{2,1,0:T(8,128)S(1)}, f32[64,128]{1,0:T(8,128)S(1)}, s32[8,256]{1,0:T(8,128)S(1)}) custom-call(f32[3,16,16,128]{3,2,1,0:T(8,128)S(1)} %copy-done, f32[3,256,128]{2,1,0:T(8,128)S(1)} %bitcast.10, f32[256,128]{1,0:T(8,128)S(1)} %copy-done.3, s32[256,128]{1,0:T(8,128)S(1)} %copy-done.4, s32[1,256]{1,0:T(1,128)S(1)} %bitcast.13, ...), custom_call_target="tpu_custom_call" | custom-call | tf_op jit(solution)/shard_map/exchange/pallas_call | solution.py:456
  105.9 5.2 %copy.31 = f32[5,18,18,128]{3,2,1,0:T(8,128)S(1)} copy(f32[5,18,18,128]{2,1,3,0:T(8,128)} %copy-done.9) | data formatting | bytes 1658880 | tf_op jit(solution)/shard_map/concatenate | solution.py:343
  111.1 0.0 collective-permute-done.4
  111.1 0.7 copy.30
  111.8 0.0 collective-permute-done.5
  111.8 1.7 %copy.33 = f32[5,18,18,1]{3,2,1,0:T(8,128)} copy(f32[5,18,18,1]{2,1,3,0:T(8,128)S(1)} %collective-permute-done.5) | data formatting | bytes 12960 | tf_op jit(solution)/shard_map/ppermute | solution.py:347
  113.4 1.2 pad_maximum_fusion.3
  114.6 0.1 copy-done.10
  114.8 4.8 %add_multiply_fusion.23 = (f32[1,17,17,129]{3,2,1,0:T(8,128)S(1)}, f32[1,17,17,129]{3,2,1,0:T(8,128)S(1)}, f32[1,17,17,129]{3,2,1,0:T(8,128)S(1)}, f32[1,17,17,1...) fusion(f32[5,18,18,128]{3,2,1,0:T(8,128)S(1)} %copy.31, ...), kind=kLoop, calls=%fused_computation.112 | loop fusion | flops 7903572 | bytes 3527050 | tf_op jit(solution)/shard_map/mul | solution.py:392
  119.6 0.5 add_multiply_fusion.22
  120.1 0.9 add_multiply_fusion.20
  121.0 0.6 fusion.31
  121.6 6.9 %scatter.1 = (f32[3,256,128]{2,1,0:T(8,128)}, f32[3,256,128]{2,1,0:T(8,128)}) custom-call(f32[64,24,128]{2,1,0:T(8,128)S(1)} %get-tuple-element.7.push, f32[64,128]{1,0:T(8,128)S(1)} %get-tuple-element.8.total, s32[8,256]{1,0:T(8,128)S(1)} %get-tuple-element.9.place, s32[64,128]{1,0:T(8,128)S(1)} %copy-done.5, f32[3,64,128]{2,1,0:T(8,128)S(1)} %bitcast.12, ...), custom_call_target="tpu_custom_call" | custom-call | tf_op jit(solution)/shard_map/scatter/pallas_call | solution.py:496
  (9 shorter events, 0.0 us)
Async XLA Ops:
  1.5 5.4 %collective-permute-start = (f32[5,1,16,128]{3,2,1,0:T(8,128)S(1)}, f32[5,1,16,128]{3,2,1,0:T(8,128)S(1)}, u32[]{:S(2)}, u32[]{:S(2)}) collective-permute-start(f32[5,1,16,128]{3,2,1,0:T(8,128)S(1)} %get-tuple-element.64), channel_id=1, source_target_pairs={{0,64},{64,128},{128,192},{1,65},{65,129},{129,193},{2,66},{66,130... | collective-permute-start | bytes 122888 | tf_op jit(solution)/shard_map/ppermute | solution.py:345
  5.5 4.7 %collective-permute-start.1 = (f32[5,1,16,128]{3,2,1,0:T(8,128)S(1)}, f32[5,1,16,128]{3,2,1,0:T(8,128)S(1)}, u32[]{:S(2)}, u32[]{:S(2)}) collective-permute-start(f32[5,1,16,128]{3,2,1,0:T(8,128)S(1)} %get-tuple-element.65), channel_id=1, source_target_pairs={{64,0},{128,64},{192,128},{65,1},{129,65},{193,129},{66,2},{130,66... | collective-permute-start | bytes 122888 | tf_op jit(solution)/shard_map/ppermute | solution.py:347
  11.5 12.0 %collective-permute-start.2 = (f32[5,18,1,128]{3,1,2,0:T(8,128)S(1)}, f32[5,18,1,128]{3,1,2,0:T(8,128)S(1)}, u32[]{:S(2)}, u32[]{:S(2)}) collective-permute-start(f32[5,18,1,128]{3,1,2,0:T(8,128)S(1)} %copy.34), channel_id=1, source_target_pairs={{0,8},{8,16},{16,24},{24,32},{32,40},{40,48},{48,56},{1,9},{9,17},... | collective-permute-start | bytes 138248 | tf_op jit(solution)/shard_map/ppermute | solution.py:345
  16.7 11.7 %collective-permute-start.3 = (f32[5,18,1,128]{3,1,2,0:T(8,128)S(1)}, f32[5,18,1,128]{3,1,2,0:T(8,128)S(1)}, u32[]{:S(2)}, u32[]{:S(2)}) collective-permute-start(f32[5,18,1,128]{3,1,2,0:T(8,128)S(1)} %copy.35), channel_id=1, source_target_pairs={{8,0},{16,8},{24,16},{32,24},{40,32},{48,40},{56,48},{9,1},{17,9},... | collective-permute-start | bytes 138248 | tf_op jit(solution)/shard_map/ppermute | solution.py:347
  33.1 15.2 %copy-start = (f32[3,16,16,128]{3,2,1,0:T(8,128)S(1)}, f32[3,16,16,128]{3,2,1,0:T(8,128)}, u32[]{:S(2)}) copy-start(f32[3,16,16,128]{3,2,1,0:T(8,128)} %disp.1) | copy-start | bytes 1179652
  33.1 15.2 %copy-start.1 = (f32[256,3,128]{2,0,1:T(8,128)S(1)}, f32[256,3,128]{2,0,1:T(8,128)}, u32[]{:S(2)}) copy-start(f32[256,3,128]{2,0,1:T(8,128)} %param.14) | copy-start | bytes 1179652
  33.1 15.2 %copy-start.2 = (f32[64,3,128]{2,0,1:T(8,128)S(1)}, f32[64,3,128]{2,0,1:T(8,128)}, u32[]{:S(2)}) copy-start(f32[64,3,128]{2,0,1:T(8,128)} %param.20) | copy-start | bytes 294916
  33.1 15.2 %copy-start.3 = (f32[256,128]{1,0:T(8,128)S(1)}, f32[256,128]{1,0:T(8,128)}, u32[]{:S(2)}) copy-start(f32[256,128]{1,0:T(8,128)} %sstiff.1) | copy-start | bytes 393220
  33.1 15.2 %copy-start.4 = (s32[256,128]{1,0:T(8,128)S(1)}, s32[256,128]{1,0:T(8,128)}, u32[]{:S(2)}) copy-start(s32[256,128]{1,0:T(8,128)} %sactive.1) | copy-start | bytes 393220
  33.1 15.2 %copy-start.5 = (s32[64,128]{1,0:T(8,128)S(1)}, s32[64,128]{1,0:T(8,128)}, u32[]{:S(2)}) copy-start(s32[64,128]{1,0:T(8,128)} %mnode.3) | copy-start | bytes 98308
  33.2 15.2 %copy-start.6 = (s32[64,128]{1,0:T(8,128)S(1)}, s32[64,128]{1,0:T(8,128)}, u32[]{:S(2)}) copy-start(s32[64,128]{1,0:T(8,128)} %factive.1) | copy-start | bytes 98308
  33.2 15.2 %copy-start.7 = (s32[256,1]{0,1:T(1,128)S(1)}, s32[256,1]{0,1:T(1,128)}, u32[]{:S(2)}) copy-start(s32[256,1]{0,1:T(1,128)} %param.17) | copy-start | bytes 3076
  33.2 15.2 %copy-start.8 = (s32[256,1]{0,1:T(1,128)S(1)}, s32[256,1]{0,1:T(1,128)}, u32[]{:S(2)}) copy-start(s32[256,1]{0,1:T(1,128)} %param.18) | copy-start | bytes 3076
  43.2 5.1 %copy-start.9 = (f32[5,18,18,128]{2,1,3,0:T(8,128)}, f32[5,18,18,128]{2,1,3,0:T(8,128)S(1)}, u32[]{:S(2)}) copy-start(f32[5,18,18,128]{2,1,3,0:T(8,128)S(1)} %pad_maximum_fusion) | copy-start | bytes 2488324
  43.2 67.9 %collective-permute-start.4 = (f32[5,18,18,1]{2,1,3,0:T(8,128)S(1)}, f32[5,18,18,1]{2,1,3,0:T(8,128)S(1)}, u32[]{:S(2)}, u32[]{:S(2)}) collective-permute-start(f32[5,18,18,1]{2,1,3,0:T(8,128)S(1)} %get-tuple-element.35), channel_id=1, source_target_pairs={{0,1},{1,2},{2,3},{3,4},{4,5},{5,6},{6,7},{8,9},{9,10},{10,11},{11... | collective-permute-start | bytes 19448 | tf_op jit(solution)/shard_map/ppermute | solution.py:345
  46.8 65.0 %collective-permute-start.5 = (f32[5,18,18,1]{2,1,3,0:T(8,128)S(1)}, f32[5,18,18,1]{2,1,3,0:T(8,128)S(1)}, u32[]{:S(2)}, u32[]{:S(2)}) collective-permute-start(f32[5,18,18,1]{2,1,3,0:T(8,128)S(1)} %get-tuple-element.34), channel_id=1, source_target_pairs={{1,0},{2,1},{3,2},{4,3},{5,4},{6,5},{7,6},{9,8},{10,9},{11,10},{12... | collective-permute-start | bytes 19448 | tf_op jit(solution)/shard_map/ppermute | solution.py:347
  113.4 1.3 %copy-start.10 = (f32[5,18,18,1]{3,2,1,0:T(8,128)S(1)}, f32[5,18,18,1]{3,2,1,0:T(8,128)}, u32[]{:S(2)}) copy-start(f32[5,18,18,1]{3,2,1,0:T(8,128)} %copy.33) | copy-start | bytes 19444

commit v2 on v1

--- a/solution.py
+++ b/solution.py
@@ -17,16 +17,6 @@
 LANES = 128
 
 gamma_gas = 5.0 / 3.0
-corner_offsets = [
-    (0, 0, 0),
-    (0, 0, 1),
-    (0, 1, 0),
-    (0, 1, 1),
-    (1, 0, 0),
-    (1, 0, 1),
-    (1, 1, 0),
-    (1, 1, 1),
-]
 
 
 def split3(x):
@@ -103,10 +93,184 @@
     return push[:24] + push[32:56], jnp.transpose(jnp.concatenate(columns, axis=1))
 
 
+def cross_parts(left, right):
+    return [
+        left[1] * right[2] - left[2] * right[1],
+        left[2] * right[0] - left[0] * right[2],
+        left[0] * right[1] - left[1] * right[0],
+    ]
+
+
+def z_and_y_sums(near, far, rows):
+    total, change = near + far, far - near
+    total_up = pltpu.roll(total, rows - 1, 0)
+    change_up = pltpu.roll(change, rows - 1, 0)
+    return total + total_up, total_up - total, change + change_up
+
+
+def zone_terms(low, high, mass, energy, valid):
+    edge_x = [0.25 * (high[c][0] - low[c][0]) + (1.0 if c == 0 else 0.0) for c in range(3)]
+    edge_y = [0.25 * (low[c][1] + high[c][1]) + (1.0 if c == 1 else 0.0) for c in range(3)]
+    edge_z = [0.25 * (low[c][2] + high[c][2]) + (1.0 if c == 2 else 0.0) for c in range(3)]
+    across_yz = cross_parts(edge_y, edge_z)
+    across_zx = cross_parts(edge_z, edge_x)
+    across_xy = cross_parts(edge_x, edge_y)
+    volume = edge_x[0] * across_yz[0] + edge_x[1] * across_yz[1] + edge_x[2] * across_yz[2]
+    pressure = jnp.where(
+        valid, (gamma_gas - 1.0) * mass * energy / jnp.where(valid, volume, 1.0), 0.0
+    )
+    quarter = 0.25 * pressure
+    return [[quarter * part for part in parts] for parts in (across_yz, across_zx, across_xy)]
+
+
+class Halo:
+    def __init__(self, disp, mass, energy, held, y_send, y_recv, z_send, z_recv, sems, sizes):
+        self.disp, self.mass, self.energy, self.held = disp, mass, energy, held
+        self.y_send, self.y_recv, self.z_send, self.z_recv = y_send, y_recv, z_send, z_recv
+        self.sems, self.sizes = sems, sizes
+        self.at = [lax.axis_index(axis) for axis in ("gx", "gy", "gz")]
+        self.cells_x, self.cells_y = disp.shape[1], disp.shape[2]
+        self.rows = held.shape[2]
+
+    def beside(self, axis, shift):
+        place = list(self.at)
+        place[axis] = lax.rem(place[axis] + self.sizes[axis] + shift, self.sizes[axis])
+        return tuple(place)
+
+    def copy(self, number, source, target, axis, shift):
+        return pltpu.make_async_remote_copy(
+            src_ref=source,
+            dst_ref=target,
+            send_sem=self.sems.at[0, number],
+            recv_sem=self.sems.at[1, number],
+            device_id=self.beside(axis, shift),
+            device_id_type=MESH,
+        )
+
+    def x_copies(self):
+        last, own = self.cells_x - 1, pl.ds(0, self.cells_y)
+        return [
+            self.copy(0, self.disp.at[:, last], self.held.at[pl.ds(0, 3), 0, own], 0, 1),
+            self.copy(1, self.mass.at[last], self.held.at[3, 0, own], 0, 1),
+            self.copy(2, self.energy.at[last], self.held.at[4, 0, own], 0, 1),
+            self.copy(3, self.disp.at[:, 0], self.held.at[pl.ds(0, 3), last + 2, own], 0, -1),
+        ]
+
+    def y_copies(self):
+        return [
+            self.copy(4, self.y_send.at[pl.ds(0, 5)], self.y_recv.at[pl.ds(0, 5)], 1, 1),
+            self.copy(5, self.y_send.at[pl.ds(5, 3)], self.y_recv.at[pl.ds(5, 3)], 1, -1),
+        ]
+
+    def z_copies(self):
+        return [
+            self.copy(6, self.z_send.at[0], self.z_recv.at[0], 2, 1),
+            self.copy(7, self.z_send.at[1], self.z_recv.at[1], 2, -1),
+        ]
+
+    def own_part(self):
+        inner = self.cells_y
+        for f in range(5):
+            source = self.disp.at[f] if f < 3 else (self.mass, self.energy)[f - 3]
+            self.held[f, :, inner:, :] = jnp.zeros(
+                (self.cells_x + 2, self.rows - inner, LANES), f32
+            )
+            self.held[f, 1 : self.cells_x + 1, 0:inner, :] = source[...]
+
+    def y_start(self):
+        slabs = self.cells_x + 2
+        for f in range(5):
+            for i in range(slabs):
+                self.y_send[f, i : i + 1, :] = self.held[f, i, self.cells_y - 1 : self.cells_y, :]
+                if f < 3:
+                    self.y_send[5 + f, i : i + 1, :] = self.held[f, i, 0:1, :]
+        for copy in self.y_copies():
+            copy.start()
+
+    def z_start(self):
+        slabs, rows = self.cells_x + 2, self.rows
+        lane = iota((rows, LANES), 1)
+        up, down = jnp.zeros((rows, LANES), f32), jnp.zeros((rows, LANES), f32)
+        for f in range(5):
+            for i in range(slabs):
+                self.held[f, i, rows - 1 : rows, :] = self.y_recv[f, i : i + 1, :]
+                if f < 3:
+                    self.held[f, i, self.cells_y : self.cells_y + 1, :] = self.y_recv[
+                        5 + f, i : i + 1, :
+                    ]
+                slab = self.held[f, i]
+                up = jnp.where(lane == f * 24 + i, slab[:, LANES - 1 : LANES], up)
+                if f < 3:
+                    down = jnp.where(lane == f * 24 + i, slab[:, 0:1], down)
+        self.z_send[0] = up
+        self.z_send[1] = down
+        for copy in self.z_copies():
+            copy.start()
+
+    def zone_forces(self, out):
+        rows, cells_x, cells_y = self.rows, self.cells_x, self.cells_y
+        lane, row = iota((rows, LANES), 1), iota((rows, LANES), 0)
+        limits = [
+            self.sizes[0] * cells_x - 2,
+            self.sizes[1] * cells_y - 2,
+            self.sizes[2] * LANES - 2,
+        ]
+        at_x = self.at[0] * cells_x
+        at_y = self.at[1] * cells_y + jnp.where(row < cells_y, row, row - rows)
+        at_z = self.at[2] * LANES + lane
+        inside_y = (at_y >= 0) & (at_y <= limits[1])
+        inside_yz = inside_y & (at_z <= limits[2])
+
+        def packed(plane, f):
+            return plane if f == 0 else pltpu.roll(plane, LANES - 24 * f, 1)
+
+        below, own = self.z_recv[0], self.z_send[1]
+        low = [z_and_y_sums(packed(below, c), packed(own, c), rows) for c in range(3)]
+        high = [[pltpu.roll(part, LANES - 1, 1) for part in parts] for parts in low]
+        i_at = at_x + lane - 1
+        valid = inside_y & (i_at >= 0) & (i_at <= limits[0]) & (self.at[2] > 0)
+        thin = zone_terms(low, high, packed(below, 3), packed(below, 4), valid)
+
+        above = self.z_recv[1]
+
+        def slab_sums(i):
+            sums = []
+            for c in range(3):
+                near = self.held[c, i]
+                q = c * 24 + i
+                far = jnp.where(
+                    lane == LANES - 1, above[:, q : q + 1], pltpu.roll(near, LANES - 1, 1)
+                )
+                sums.append(z_and_y_sums(near, far, rows))
+            return sums
+
+        low = slab_sums(0)
+        for i in range(cells_x + 1):
+            high = slab_sums(i + 1)
+            i_at = at_x + (i - 1)
+            valid = inside_yz & (i_at >= 0) & (i_at <= limits[0])
+            terms = zone_terms(low, high, self.held[3, i], self.held[4, i], valid)
+            for c in range(3):
+                here = [terms[a][c] for a in range(3)]
+                back = [
+                    jnp.where(lane == 0, thin[a][c][:, i : i + 1], pltpu.roll(here[a], 1, 1))
+                    for a in range(3)
+                ]
+                sum_x, sum_y, sum_z = here[0] + back[0], here[1] + back[1], back[2] - here[2]
+                along = sum_x + pltpu.roll(sum_x, 1, 0)
+                aside = pltpu.roll(sum_y + sum_z, 1, 0) + (sum_z - sum_y)
+                if i < cells_x:
+                    out[c, i * cells_y : (i + 1) * cells_y, :] = (aside + along)[0:cells_y]
+                if i > 0:
+                    out[c, (i - 1) * cells_y : i * cells_y, :] += (aside - along)[0:cells_y]
+            low = high
+
+
 def exchange_kernel(
-    size_y,
-    size_z,
+    sizes,
     disp,
+    mass,
+    energy,
     spos,
     sstiff,
     sactive,
@@ -118,6 +282,7 @@
     push_out,
     total_out,
     place_out,
+    zone_out,
     ask_send,
     ask_recv,
     give_send,
@@ -128,10 +293,18 @@
     centers,
     table,
     hot_t,
+    held,
+    y_send,
+    y_recv,
+    z_send,
+    z_recv,
     ask_sems,
     give_sems,
     back_sems,
+    halo_sems,
 ):
+    size_y, size_z = sizes[1:]
+    halo = Halo(disp, mass, energy, held, y_send, y_recv, z_send, z_recv, halo_sems, sizes)
     peers = size_y * size_z
     count = peer.shape[1]
     masters = mnode.shape[0]
@@ -154,6 +327,10 @@
         return carry
 
     lax.fori_loop(1, peers, greet, 0)
+    for shift in (1, -1):
+        pl.semaphore_signal(
+            barrier, inc=1, device_id=halo.beside(0, shift), device_id_type=MESH
+        )
 
     named = peer[...]
     ahead = lax.rem(named // size_z - gy + size_y, size_y) * size_z + lax.rem(
@@ -172,7 +349,7 @@
         ask_send[t] = asked[t : t + 1, :]
     ask_recv[0] = asked[0:1, :]
 
-    pl.semaphore_wait(barrier, peers - 1)
+    pl.semaphore_wait(barrier, peers + 1)
 
     def ask_copy(t):
         return pltpu.make_async_remote_copy(
@@ -209,6 +386,9 @@
         return carry
 
     lax.fori_loop(1, peers, ask_start, 0)
+    for copy in halo.x_copies():
+        copy.start()
+    halo.own_part()
 
     gather_centers(disp, mnode, centers, table)
     live = factive[...].astype(f32)
@@ -216,6 +396,10 @@
     moved = areas[0] * centers[0] + areas[1] * centers[1] + areas[2] * centers[2]
     pack = jnp.concatenate(areas + [moved], axis=1)
     pack3 = jnp.concatenate(split3(pack), axis=0)
+
+    for copy in halo.x_copies():
+        copy.wait_recv()
+    halo.y_start()
 
     def ask_wait(t, carry):
         ask_copy(t).wait_recv()
@@ -244,6 +428,9 @@
 
     lax.fori_loop(1, peers, give_start, 0)
     give_recv[0] = give_send[0]
+    for copy in halo.y_copies():
+        copy.wait_recv()
+    halo.z_start()
 
     stiff = sstiff[...] * sactive[...].astype(f32)
     slots = (place == iota((peers * SLOTS, count), 0)).astype(f32).astype(bf16)
@@ -253,6 +440,10 @@
         rows = dot(slots, parts[0]) + dot(slots, parts[1]) + dot(slots, parts[2])
         slave[:, c * SLOTS : (c + 1) * SLOTS, :] = rows.reshape(peers, SLOTS, LANES)
 
+    for copy in halo.z_copies():
+        copy.wait_recv()
+    halo.zone_forces(zone_out)
+
     step_of = 4
 
     def contact(q, carry):
@@ -288,6 +479,8 @@
         return carry
 
     lax.fori_loop(1, peers, finish, 0)
+    for copy in halo.x_copies() + halo.y_copies() + halo.z_copies():
+        copy.wait_send()
     parts = split3(back_recv[...].reshape(peers * SLOTS, LANES))
     turned = hot_t[0:masters, :]
     total_out[...] = dot(turned, parts[0]) + dot(turned, parts[1]) + dot(turned, parts[2])
@@ -334,104 +527,6 @@
         node_out[c] = zone[c] + jnp.transpose(grid[c * LANES : (c + 1) * LANES, :])
 
 
-def extended_2(cells, sides, width):
-    for axis, dim in sides:
-        count = lax.axis_size(axis)
-        ends = count - 1
-        head = lax.slice_in_dim(cells, 0, width, axis=dim)
-        tail = lax.slice_in_dim(cells, cells.shape[dim] - width, cells.shape[dim], axis=dim)
-        cells = jnp.concatenate(
-            [
-                lax.ppermute(tail, axis, [(i, (i + 1) % count) for i in range(ends)]),
-                cells,
-                lax.ppermute(head, axis, [((i + 1) % count, i) for i in range(ends)]),
-            ],
-            axis=dim,
-        )
-    return cells
-
-
-def cross_parts(left, right):
-    return [
-        left[1] * right[2] - left[2] * right[1],
-        left[2] * right[0] - left[0] * right[2],
-        left[0] * right[1] - left[1] * right[0],
-    ]
-
-
-def zone_state(corner_moves, masses, energies, valid):
-    edges = []
-    for axis_pick in range(3):
-        parts = []
-        for comp in range(3):
-            total = jnp.zeros_like(masses)
-            for moved, offset in zip(corner_moves, corner_offsets):
-                total = total + (2.0 * offset[axis_pick] - 1.0) * moved[comp]
-            total = total * 0.25
-            if comp == axis_pick:
-                total = total + 1.0
-            parts.append(total)
-        edges.append(parts)
-    cross_yz = cross_parts(edges[1], edges[2])
-    cross_zx = cross_parts(edges[2], edges[0])
-    cross_xy = cross_parts(edges[0], edges[1])
-    volume = edges[0][0] * cross_yz[0] + edges[0][1] * cross_yz[1] + edges[0][2] * cross_yz[2]
-    pressure = jnp.where(
-        valid, (gamma_gas - 1.0) * masses * energies / jnp.where(valid, volume, 1.0), 0.0
-    )
-    return (pressure, cross_yz, cross_zx, cross_xy)
-
-
-def corner_force(state, offset):
-    pressure, cross_yz, cross_zx, cross_xy = state
-    sign_x = 2.0 * offset[0] - 1.0
-    sign_y = 2.0 * offset[1] - 1.0
-    sign_z = 2.0 * offset[2] - 1.0
-    return jnp.stack(
-        [
-            pressure
-            * 0.25
-            * (sign_x * cross_yz[comp] + sign_y * cross_zx[comp] + sign_z * cross_xy[comp])
-            for comp in range(3)
-        ]
-    )
-
-
-def axis_valid(position, count, length):
-    global_row = position * count + jnp.arange(count + 1, dtype=jnp.int32) - 1
-    return (global_row >= 0) & (global_row <= length - 2)
-
-
-def zone_part(displacement, zone_mass, zone_energy):
-    cells_x, cells_y, cells_z = (
-        displacement.shape[1],
-        displacement.shape[2],
-        displacement.shape[3],
-    )
-    fields = jnp.concatenate([displacement, zone_mass[None], zone_energy[None]], axis=0)
-    extended = extended_2(fields, (("gx", 1), ("gy", 2), ("gz", 3)), 1)
-    valid_x = axis_valid(lax.axis_index("gx"), cells_x, cells_x * lax.axis_size("gx"))
-    valid_y = axis_valid(lax.axis_index("gy"), cells_y, cells_y * lax.axis_size("gy"))
-    valid_z = axis_valid(lax.axis_index("gz"), cells_z, cells_z * lax.axis_size("gz"))
-    valid = valid_x[:, None, None] & valid_y[None, :, None] & valid_z[None, None, :]
-    corner_moves = [
-        extended[0:3, a : a + cells_x + 1, b : b + cells_y + 1, e : e + cells_z + 1]
-        for a, b, e in corner_offsets
-    ]
-    masses = extended[3, : cells_x + 1, : cells_y + 1, : cells_z + 1]
-    energies = extended[4, : cells_x + 1, : cells_y + 1, : cells_z + 1]
-    state = zone_state(corner_moves, masses, energies, valid)
-    node_force = jnp.zeros((3, cells_x, cells_y, cells_z), jnp.float32)
-    for offset in corner_offsets:
-        a, b, e = offset
-        forces = corner_force(state, offset)
-        node_force = (
-            node_force
-            + forces[:, 1 - a : 1 - a + cells_x, 1 - b : 1 - b + cells_y, 1 - e : 1 - e + cells_z]
-        )
-    return node_force
-
-
 def body(
     displacement,
     zone_mass,
@@ -445,23 +540,23 @@
     master_area,
     face_active,
 ):
-    size_y = lax.axis_size("gy")
-    size_z = lax.axis_size("gz")
-    peers = size_y * size_z
+    sizes = tuple(lax.axis_size(axis) for axis in ("gx", "gy", "gz"))
+    peers = sizes[1] * sizes[2]
     count = slave_position.shape[0]
     masters = master_node.shape[0]
     cells = displacement.shape[1:]
     rows = cells[0] * cells[1]
     area = jnp.transpose(master_area, (1, 0, 2))
-    push, total, place = pl.pallas_call(
-        functools.partial(exchange_kernel, size_y, size_z),
+    push, total, place, zone = pl.pallas_call(
+        functools.partial(exchange_kernel, sizes),
         out_shape=(
             jax.ShapeDtypeStruct((peers, 24, LANES), f32),
             jax.ShapeDtypeStruct((masters, LANES), f32),
             jax.ShapeDtypeStruct((8, count), i32),
+            jax.ShapeDtypeStruct((3, rows, LANES), f32),
         ),
-        in_specs=[VMEM] * 9,
-        out_specs=(VMEM,) * 3,
+        in_specs=[VMEM] * 11,
+        out_specs=(VMEM,) * 4,
         scratch_shapes=[
             pltpu.VMEM((peers, 1, LANES), f32),
             pltpu.VMEM((peers, 1, LANES), f32),
@@ -473,9 +568,15 @@
             pltpu.VMEM((3, masters, LANES), f32),
             pltpu.VMEM((3 * LANES, 3 * rows), bf16),
             pltpu.VMEM((LANES, peers * SLOTS), bf16),
+            pltpu.VMEM((5, cells[0] + 2, cells[1] + 8, LANES), f32),
+            pltpu.VMEM((8, cells[0] + 8, LANES), f32),
+            pltpu.VMEM((8, cells[0] + 8, LANES), f32),
+            pltpu.VMEM((2, cells[1] + 8, LANES), f32),
+            pltpu.VMEM((2, cells[1] + 8, LANES), f32),
             pltpu.SemaphoreType.DMA((2, peers)),
             pltpu.SemaphoreType.DMA((2, peers)),
             pltpu.SemaphoreType.DMA((2, peers)),
+            pltpu.SemaphoreType.DMA((2, 8)),
         ],
         compiler_params=pltpu.CompilerParams(
             collective_id=0, has_side_effects=True, vmem_limit_bytes=48 * 2**20
@@ -483,6 +584,8 @@
         name="exchange",
     )(
         displacement,
+        zone_mass,
+        zone_energy,
         jnp.transpose(slave_position, (1, 0, 2)),
         slave_stiffness,
         slave_active,
@@ -492,7 +595,6 @@
         area,
         face_active,
     )
-    zone = zone_part(displacement, zone_mass, zone_energy)
     node_force, slave_force = pl.pallas_call(
         scatter_kernel,
         out_shape=(
@@ -504,7 +606,7 @@
         scratch_shapes=[pltpu.VMEM((3 * LANES, rows), f32)],
         compiler_params=pltpu.CompilerParams(vmem_limit_bytes=48 * 2**20),
         name="scatter",
-    )(push, total, place, master_node, area, zone.reshape(3, rows, LANES))
+    )(push, total, place, master_node, area, zone)
     return (
         node_force.reshape((3,) + cells),
         jnp.transpose(slave_force, (1, 0, 2)),

time: 129 us -> 94 us (0.73)
  other arithmetic: 20.1 us -> 0 us
  Pallas kernels: 64.5 us -> 84.2 us
  starting transfers between devices: 17.4 us -> 0 us
  local copies, waits for them, and re-layouts: 22.2 us -> 8.69 us
  waiting for transfers between devices: 3.43 us -> 0 us
    pallas_call x1, Pallas kernels: 57.5 us -> 77.3 us  [body(): pl.pallas_call(functools.partial(exchange_kernel, sizes), out_shape=(jax....]
    ppermute x6 -> x0, starting transfers between devices: 17.4 us -> none  [the longest x3 12.7 us: extended_2(): lax.ppermute(tail, axis, [(i, (i + 1) % count) for i in range(ends)])]
    concatenate x3 -> x0, other arithmetic: 12.4 us -> none  [extended_2(): jnp.concatenate([lax.ppermute(tail, axis, [(i, (i + 1) % count) for i in...]
    ppermute x4 -> x0, local copies, waits for them, and re-layouts: 11.9 us -> none  [the longest x2 6.41 us: extended_2(): lax.ppermute(head, axis, [((i + 1) % count, i) for i in range(ends)])]
    concatenate x2 -> x0, local copies, waits for them, and re-layouts: 10.1 us -> none  [extended_2(): jnp.concatenate([lax.ppermute(tail, axis, [(i, (i + 1) % count) for i in...]
    unnamed x24 -> x22, local copies, waits for them, and re-layouts: 0.2 us -> 8.69 us
    mul x3 -> x0, other arithmetic: 6.22 us -> none  [corner_force(): pressure * 0.25]
    ppermute x6 -> x0, waiting for transfers between devices: 3.43 us -> none  [the longest x3 3.42 us: extended_2(): lax.ppermute(head, axis, [((i + 1) % count, i) for i in range(ends)])]
  transfers between devices with their start and end apart: 6 -> 0, of which waited for: 1 -> 0; matrix products, arithmetic and copies ran while one was open for 12% -> 0% of each run, Pallas kernels for 45% -> 0%
where the time goes in v2:
time: 94 us; the launch traced here: 93.6 us
  Pallas kernels  84.2 us (90%)
  local copies, waits for them, and re-layouts  8.69 us (9%)
    pallas_call x1, Pallas kernels, body(): pl.pallas_call(functools.partial(exchange_kernel, sizes), out_shape=(jax....  77.3 us
    unnamed x22, local copies, waits for them, and re-layouts  8.69 us
    pallas_call x1, Pallas kernels, body(): pl.pallas_call(scatter_kernel, out_shape=(jax.ShapeDtypeStruct((3, rows,...  6.93 us

profile of v2, /device:TPU:1, one launch (start us, length us, event | category | flops | bytes accessed | tf_op | source)
XLA Modules:
  0.0 93.6 jit_solution(8674943760353215416)
XLA Ops:
  0.6 0.0 copy-start.10
  0.6 0.0 copy-start.9
  0.7 0.7 copy-done.10
  1.3 0.0 copy-done.9
  1.3 0.0 copy-start
  1.3 1.0 %copy-done = f32[3,16,16,128]{3,2,1,0:T(8,128)S(1)} copy-done((f32[3,16,16,128]{3,2,1,0:T(8,128)S(1)}, f32[3,16,16,128]{3,2,1,0:T(8,128)}, u32[]{:S(2)}) %copy-start) | copy-done | bytes 393240
  2.3 0.0 copy-start.1
  2.3 1.0 %copy-done.1 = f32[256,3,128]{2,0,1:T(8,128)S(1)} copy-done((f32[256,3,128]{2,0,1:T(8,128)S(1)}, f32[256,3,128]{2,0,1:T(8,128)}, u32[]{:S(2)}) %copy-start.1) | copy-done | bytes 393240
  3.3 0.0 copy-start.2
  3.3 0.9 copy-done.2
  4.2 0.0 copy-start.3
  4.2 0.9 copy-done.3
  5.1 0.0 copy-start.4
  5.1 0.9 copy-done.4
  6.0 0.0 copy-start.5
  6.0 0.9 copy-done.5
  6.9 0.0 copy-start.6
  6.9 0.9 copy-done.6
  7.8 0.0 copy-start.7
  7.8 0.8 copy-done.7
  8.6 0.0 copy-start.8
  8.6 0.8 copy-done.8
  9.4 77.3 %exchange.1 = (f32[64,24,128]{2,1,0:T(8,128)S(1)}, f32[64,128]{1,0:T(8,128)S(1)}, s32[8,256]{1,0:T(8,128)S(1)}, f32[3,256,128]{2,1,0:T(8,128)S(1)}) custom-call(f32[3,16,16,128]{3,2,1,0:T(8,128)S(1)} %copy-done, f32[16,16,128]{2,1,0:T(8,128)S(1)} %copy-done.3, f32[16,16,128]{2,1,0:T(8,128)S(1)} %copy-done.4, f32[3,256,128]{2,1,0:T(8,128)S(1)} %bitcast.6, ...), custom_call_target="tpu_custom_call" | custom-call | tf_op jit(solution)/shard_map/exchange/pallas_call | solution.py:550
  86.6 6.9 %scatter.1 = (f32[3,256,128]{2,1,0:T(8,128)}, f32[3,256,128]{2,1,0:T(8,128)}) custom-call(f32[64,24,128]{2,1,0:T(8,128)S(1)} %get-tuple-element.8.push, f32[64,128]{1,0:T(8,128)S(1)} %get-tuple-element.9.total, s32[8,256]{1,0:T(8,128)S(1)} %get-tuple-element.10.place, s32[64,128]{1,0:T(8,128)S(1)} %copy-done.7, f32[3,64,128]{2,1,0:T(8,128)S(1)} %bitcast.8, ...), custom_call_target="tpu_custom_call" | custom-call | tf_op jit(solution)/shard_map/scatter/pallas_call | solution.py:598
Async XLA Ops:
  0.6 0.7 copy-start.10
  0.6 0.7 copy-start.9
  1.3 1.0 %copy-start = (f32[3,16,16,128]{3,2,1,0:T(8,128)S(1)}, f32[3,16,16,128]{3,2,1,0:T(8,128)}, u32[]{:S(2)}) copy-start(f32[3,16,16,128]{3,2,1,0:T(8,128)} %disp.1) | copy-start | bytes 1179652
  2.3 1.0 %copy-start.1 = (f32[256,3,128]{2,0,1:T(8,128)S(1)}, f32[256,3,128]{2,0,1:T(8,128)}, u32[]{:S(2)}) copy-start(f32[256,3,128]{2,0,1:T(8,128)} %param.14) | copy-start | bytes 1179652
  3.3 0.9 copy-start.2
  4.2 0.9 copy-start.3
  5.1 0.9 copy-start.4
  6.0 0.9 copy-start.5
  6.9 0.9 copy-start.6
  7.8 0.8 copy-start.7
  8.6 0.8 copy-start.8

commit v3 on v2

--- a/solution.py
+++ b/solution.py
@@ -13,6 +13,7 @@
 NT = (((1,), (1,)), ((), ()))
 MESH = pl.DeviceIdType.MESH
 VMEM = pl.BlockSpec(memory_space=pltpu.VMEM)
+HBM = pl.BlockSpec(memory_space=pltpu.HBM)
 SLOTS = 8
 LANES = 128
 
@@ -266,80 +267,64 @@
             low = high
 
 
-def exchange_kernel(
-    sizes,
-    disp,
-    mass,
-    energy,
-    spos,
-    sstiff,
-    sactive,
-    peer,
-    block,
-    mnode,
-    marea,
-    factive,
-    push_out,
-    total_out,
-    place_out,
-    zone_out,
-    ask_send,
-    ask_recv,
-    give_send,
-    give_recv,
-    back_send,
-    back_recv,
-    slave,
-    centers,
-    table,
-    hot_t,
-    held,
-    y_send,
-    y_recv,
-    z_send,
-    z_recv,
-    ask_sems,
-    give_sems,
-    back_sems,
-    halo_sems,
-):
+def split_refs(refs, counts):
+    groups, at = [], 0
+    for count in counts:
+        groups.append(refs[at : at + count])
+        at += count
+    return groups
+
+
+def exchange_kernel(sizes, *refs):
+    (
+        inputs,
+        (push_out, total_out, place_out, zone_out),
+        locals_,
+        (ask_send, ask_recv, packs, give_send, give_recv, back_send, back_recv, sum_send, sum_recv),
+        (slave, centers, table, hot, hot_t),
+        (held, y_send, y_recv, z_send, z_recv),
+        (in_sems, ask_sems, ring_sems, give_sems, back_sems, sum_sems, halo_sems),
+    ) = split_refs(refs, (11, 4, 11, 9, 5, 5, 7))
+    disp, mass, energy, spos, sstiff, sactive, peer, block, mnode, marea, factive = locals_
     size_y, size_z = sizes[1:]
-    halo = Halo(disp, mass, energy, held, y_send, y_recv, z_send, z_recv, halo_sems, sizes)
     peers = size_y * size_z
     count = peer.shape[1]
     masters = mnode.shape[0]
     gx, gy, gz = lax.axis_index("gx"), lax.axis_index("gy"), lax.axis_index("gz")
-
-    def device_ahead(t):
-        return (gx, lax.rem(gy + t // size_z, size_y), lax.rem(gz + t % size_z, size_z))
-
-    def device_behind(t):
-        return (
-            gx,
-            lax.rem(gy + size_y - t // size_z, size_y),
-            lax.rem(gz + size_z - t % size_z, size_z),
-        )
+    halo = Halo(disp, mass, energy, held, y_send, y_recv, z_send, z_recv, halo_sems, sizes)
+
+    def load(n):
+        return pltpu.make_async_copy(inputs[n], locals_[n], in_sems.at[n])
+
+    for n in range(11):
+        load(n).start()
+
+    def along_y(shift):
+        return (gx, lax.rem(gy + shift + size_y, size_y), gz)
+
+    def along_z(shift):
+        return (gx, gy, lax.rem(gz + shift + size_z, size_z))
 
     barrier = pltpu.get_barrier_semaphore()
-
-    def greet(t, carry):
-        pl.semaphore_signal(barrier, inc=1, device_id=device_ahead(t), device_id_type=MESH)
-        return carry
-
-    lax.fori_loop(1, peers, greet, 0)
-    for shift in (1, -1):
-        pl.semaphore_signal(
-            barrier, inc=1, device_id=halo.beside(0, shift), device_id_type=MESH
-        )
+    greeted = [along_y(n) for n in range(1, size_y)] + [along_z(n) for n in range(1, size_z)]
+    greeted += [halo.beside(0, 1), halo.beside(0, -1)]
+    for device in greeted:
+        pl.semaphore_signal(barrier, inc=1, device_id=device, device_id_type=MESH)
+
+    def z_shift(b):
+        return jnp.where(b % 2 == 1, -((b + 1) // 2), b // 2)
+
+    for n in range(11):
+        load(n).wait()
 
     named = peer[...]
-    ahead = lax.rem(named // size_z - gy + size_y, size_y) * size_z + lax.rem(
-        named % size_z - gz + size_z, size_z
-    )
-    to_peer = (ahead == iota((peers, count), 0)).astype(f32)
+    aside = lax.rem(named // size_z - gy + size_y, size_y)
+    away = lax.rem(named % size_z - gz + size_z, size_z)
+    batch = jnp.where(away < size_z // 2, 2 * away, 2 * (size_z - away) - 1)
+    to_peer = (aside * size_z + batch == iota((peers, count), 0)).astype(f32)
     before = (iota((count, count), 0) < iota((count, count), 1)).astype(f32).astype(bf16)
     rank = jnp.sum(to_peer * dot(to_peer.astype(bf16), before), axis=0, keepdims=True).astype(i32)
-    place = ahead * SLOTS + rank
+    place = (batch * size_y + aside) * SLOTS + rank
     place_out[...] = jnp.broadcast_to(place, place_out.shape)
     in_rank = jnp.where(rank == iota((LANES, count), 0), (block[...] + 1).astype(f32), 0.0)
     asked = lax.dot_general(
@@ -347,45 +332,74 @@
     )
     for t in range(peers):
         ask_send[t] = asked[t : t + 1, :]
-    ask_recv[0] = asked[0:1, :]
-
-    pl.semaphore_wait(barrier, peers + 1)
-
-    def ask_copy(t):
+    ask_recv[0:size_z] = ask_send[0:size_z]
+
+    pl.semaphore_wait(barrier, len(greeted))
+
+    def ask_copy(n):
+        rows = pl.ds(n * size_z, size_z)
         return pltpu.make_async_remote_copy(
-            src_ref=ask_send.at[t],
-            dst_ref=ask_recv.at[t],
-            send_sem=ask_sems.at[0, t],
-            recv_sem=ask_sems.at[1, t],
-            device_id=device_ahead(t),
+            src_ref=ask_send.at[rows],
+            dst_ref=ask_recv.at[rows],
+            send_sem=ask_sems.at[0, n],
+            recv_sem=ask_sems.at[1, n],
+            device_id=along_y(n),
             device_id_type=MESH,
         )
 
-    def give_copy(t):
+    half = masters // 2
+
+    def ring_copy(step, up):
+        side = 0 if up else 1
+        source = 0 if step == 0 else 2 * step - 1 + side
+        target = 2 * step + 1 + side
+        if step == size_z // 2 - 1:
+            rows, target = pl.ds(side * half, half), size_z - 1
+        else:
+            rows = pl.ds(0, masters)
+        return pltpu.make_async_remote_copy(
+            src_ref=packs.at[source, rows],
+            dst_ref=packs.at[target, rows],
+            send_sem=ring_sems.at[0, side, step],
+            recv_sem=ring_sems.at[1, side, step],
+            device_id=along_z(1 if up else -1),
+            device_id_type=MESH,
+        )
+
+    def give_copy(b, n):
+        t = b * size_y + n
         return pltpu.make_async_remote_copy(
             src_ref=give_send.at[t],
             dst_ref=give_recv.at[t],
             send_sem=give_sems.at[0, t],
             recv_sem=give_sems.at[1, t],
-            device_id=device_behind(t),
+            device_id=along_y(-n),
             device_id_type=MESH,
         )
 
-    def back_copy(t):
+    def back_copy(b, n):
+        t = b * size_y + n
         return pltpu.make_async_remote_copy(
             src_ref=back_send.at[t],
             dst_ref=back_recv.at[t],
             send_sem=back_sems.at[0, t],
             recv_sem=back_sems.at[1, t],
-            device_id=device_ahead(t),
+            device_id=along_y(n),
             device_id_type=MESH,
         )
 
-    def ask_start(t, carry):
-        ask_copy(t).start()
-        return carry
-
-    lax.fori_loop(1, peers, ask_start, 0)
+    def sum_copy(b):
+        return pltpu.make_async_remote_copy(
+            src_ref=sum_send.at[b],
+            dst_ref=sum_recv.at[b],
+            send_sem=sum_sems.at[0, b],
+            recv_sem=sum_sems.at[1, b],
+            device_id=along_z(z_shift(b)),
+            device_id_type=MESH,
+        )
+
+    for n in range(1, size_y):
+        ask_copy(n).start()
     for copy in halo.x_copies():
         copy.start()
     halo.own_part()
@@ -394,40 +408,39 @@
     live = factive[...].astype(f32)
     areas = [marea[c] * live for c in range(3)]
     moved = areas[0] * centers[0] + areas[1] * centers[1] + areas[2] * centers[2]
-    pack = jnp.concatenate(areas + [moved], axis=1)
-    pack3 = jnp.concatenate(split3(pack), axis=0)
+    packs[0] = jnp.concatenate(areas + [moved], axis=1)
+    ring_copy(0, True).start()
+    ring_copy(0, False).start()
 
     for copy in halo.x_copies():
         copy.wait_recv()
     halo.y_start()
 
-    def ask_wait(t, carry):
-        ask_copy(t).wait_recv()
-        return carry
-
-    lax.fori_loop(1, peers, ask_wait, 0)
+    for n in range(1, size_y):
+        ask_copy(n).wait_recv()
     diagonal = (iota((peers, SLOTS, LANES), 1) == iota((peers, SLOTS, LANES), 2)).astype(f32)
     wanted = jnp.sum(
         jnp.broadcast_to(ask_recv[...], (peers, SLOTS, LANES)) * diagonal, axis=2, keepdims=True
     )
-    wanted = wanted.astype(i32).reshape(peers * SLOTS, 1) - 1
-    hot = (wanted == iota((peers * SLOTS, masters), 1)).astype(f32)
-    hot_t[...] = jnp.transpose(
-        (wanted == iota((peers * SLOTS, LANES), 1)).astype(f32)
-    ).astype(bf16)
-    hot3 = jnp.concatenate([hot, hot, hot], axis=1).astype(bf16)
-    given = dot(hot3, pack3)
-    for c in range(4):
-        give_send[:, c * SLOTS : (c + 1) * SLOTS, :] = given[
-            :, c * LANES : (c + 1) * LANES
-        ].reshape(peers, SLOTS, LANES)
-
-    def give_start(t, carry):
-        give_copy(t).start()
-        return carry
-
-    lax.fori_loop(1, peers, give_start, 0)
-    give_recv[0] = give_send[0]
+    picked = (wanted.astype(i32) - 1 == iota((peers, SLOTS, LANES), 2)).astype(f32)
+    hot[...] = picked.reshape(size_y, size_z, SLOTS, LANES)
+    for b in range(size_z):
+        chosen = hot[:, b].reshape(size_y * SLOTS, LANES)
+        hot_t[b] = jnp.transpose(chosen)[0:masters].astype(bf16)
+
+    def give(b):
+        chosen = hot[:, b].reshape(size_y * SLOTS, LANES)[:, 0:masters]
+        chosen = jnp.concatenate([chosen, chosen, chosen], axis=1).astype(bf16)
+        given = dot(chosen, jnp.concatenate(split3(packs[b]), axis=0))
+        for c in range(4):
+            give_send[b * size_y : (b + 1) * size_y, c * SLOTS : (c + 1) * SLOTS, :] = given[
+                :, c * LANES : (c + 1) * LANES
+            ].reshape(size_y, SLOTS, LANES)
+        for n in range(1, size_y):
+            give_copy(b, n).start()
+        give_recv[b * size_y] = give_send[b * size_y]
+
+    give(0)
     for copy in halo.y_copies():
         copy.wait_recv()
     halo.z_start()
@@ -444,15 +457,49 @@
         copy.wait_recv()
     halo.zone_forces(zone_out)
 
+    def ring_step(step):
+        last = step == size_z // 2 - 1
+        for up in (True, False):
+            ring_copy(step, up).wait_recv()
+            if not last:
+                ring_copy(step + 1, up).start()
+        for b in (2 * step + 1, 2 * step + 2):
+            if b < size_z:
+                give(b)
+
+    def summed(b):
+        for n in range(1, size_y):
+            back_copy(b, n).wait_recv()
+        rows = back_recv[pl.ds(b * size_y, size_y)].reshape(size_y * SLOTS, LANES)
+        parts = split3(rows)
+        turned = hot_t[b]
+        sum_send[b] = dot(turned, parts[0]) + dot(turned, parts[1]) + dot(turned, parts[2])
+
+        @pl.when(b > 0)
+        def _():
+            sum_copy(b).start()
+
     step_of = 4
+    parts_of = size_y // step_of
 
     def contact(q, carry):
+        for step in range(size_z // 2):
+
+            @pl.when(q == 3 * step)
+            def _():
+                ring_step(step)
+
+        @pl.when((q % parts_of == 0) & (q >= 2 * parts_of))
+        def _():
+            summed(q // parts_of - 2)
+
+        b = q // parts_of
         for u in range(step_of):
-            t = q * step_of + u
-
-            @pl.when(t > 0)
+            n = (q % parts_of) * step_of + u
+
+            @pl.when(n > 0)
             def _():
-                give_copy(t).wait_recv()
+                give_copy(b, n).wait_recv()
 
         for u in range(step_of):
             t = q * step_of + u
@@ -460,30 +507,42 @@
             push_out[t] = push
             back_send[t] = total
         for u in range(step_of):
-            t = q * step_of + u
-
-            @pl.when(t > 0)
+            n = (q % parts_of) * step_of + u
+
+            @pl.when(n > 0)
             def _():
-                back_copy(t).start()
+                back_copy(b, n).start()
+
+            @pl.when(n == 0)
+            def _():
+                back_recv[b * size_y] = back_send[b * size_y]
 
         return carry
 
-    lax.fori_loop(0, peers // step_of, contact, 0)
-    back_recv[0] = back_send[0]
-
-    def finish(t, carry):
-        back_copy(t).wait_recv()
-        back_copy(t).wait_send()
-        give_copy(t).wait_send()
-        ask_copy(t).wait_send()
+    lax.fori_loop(0, size_z * parts_of, contact, 0)
+    summed(size_z - 2)
+    summed(size_z - 1)
+
+    def sent(b, carry):
+        for n in range(1, size_y):
+            give_copy(b, n).wait_send()
+            back_copy(b, n).wait_send()
         return carry
 
-    lax.fori_loop(1, peers, finish, 0)
+    lax.fori_loop(0, size_z, sent, 0)
+    for n in range(1, size_y):
+        ask_copy(n).wait_send()
+    for step in range(size_z // 2):
+        ring_copy(step, True).wait_send()
+        ring_copy(step, False).wait_send()
     for copy in halo.x_copies() + halo.y_copies() + halo.z_copies():
         copy.wait_send()
-    parts = split3(back_recv[...].reshape(peers * SLOTS, LANES))
-    turned = hot_t[0:masters, :]
-    total_out[...] = dot(turned, parts[0]) + dot(turned, parts[1]) + dot(turned, parts[2])
+    total = sum_send[0]
+    for b in range(1, size_z):
+        sum_copy(b).wait_recv()
+        sum_copy(b).wait_send()
+        total = total + sum_recv[b]
+    total_out[...] = total
 
 
 def scatter_kernel(push, total, place, mnode, marea, zone, node_out, slave_out, grid):
@@ -555,27 +614,45 @@
             jax.ShapeDtypeStruct((8, count), i32),
             jax.ShapeDtypeStruct((3, rows, LANES), f32),
         ),
-        in_specs=[VMEM] * 11,
+        in_specs=[HBM] * 11,
         out_specs=(VMEM,) * 4,
         scratch_shapes=[
+            pltpu.VMEM(displacement.shape, f32),
+            pltpu.VMEM(zone_mass.shape, f32),
+            pltpu.VMEM(zone_energy.shape, f32),
+            pltpu.VMEM((3, count, LANES), f32),
+            pltpu.VMEM((count, LANES), f32),
+            pltpu.VMEM((count, LANES), i32),
+            pltpu.VMEM((1, count), i32),
+            pltpu.VMEM((1, count), i32),
+            pltpu.VMEM((masters, LANES), i32),
+            pltpu.VMEM((3, masters, LANES), f32),
+            pltpu.VMEM((masters, LANES), i32),
             pltpu.VMEM((peers, 1, LANES), f32),
             pltpu.VMEM((peers, 1, LANES), f32),
+            pltpu.VMEM((sizes[2], masters, 4 * LANES), f32),
             pltpu.VMEM((peers, 32, LANES), f32),
             pltpu.VMEM((peers, 32, LANES), f32),
             pltpu.VMEM((peers, 8, LANES), f32),
             pltpu.VMEM((peers, 8, LANES), f32),
+            pltpu.VMEM((sizes[2], masters, LANES), f32),
+            pltpu.VMEM((sizes[2], masters, LANES), f32),
             pltpu.VMEM((peers, 32, LANES), f32),
             pltpu.VMEM((3, masters, LANES), f32),
             pltpu.VMEM((3 * LANES, 3 * rows), bf16),
-            pltpu.VMEM((LANES, peers * SLOTS), bf16),
+            pltpu.VMEM((sizes[1], sizes[2], SLOTS, LANES), f32),
+            pltpu.VMEM((sizes[2], masters, sizes[1] * SLOTS), bf16),
             pltpu.VMEM((5, cells[0] + 2, cells[1] + 8, LANES), f32),
             pltpu.VMEM((8, cells[0] + 8, LANES), f32),
             pltpu.VMEM((8, cells[0] + 8, LANES), f32),
             pltpu.VMEM((2, cells[1] + 8, LANES), f32),
             pltpu.VMEM((2, cells[1] + 8, LANES), f32),
+            pltpu.SemaphoreType.DMA((11,)),
+            pltpu.SemaphoreType.DMA((2, sizes[1])),
+            pltpu.SemaphoreType.DMA((2, 2, sizes[2] // 2)),
             pltpu.SemaphoreType.DMA((2, peers)),
             pltpu.SemaphoreType.DMA((2, peers)),
-            pltpu.SemaphoreType.DMA((2, peers)),
+            pltpu.SemaphoreType.DMA((2, sizes[2])),
             pltpu.SemaphoreType.DMA((2, 8)),
         ],
         compiler_params=pltpu.CompilerParams(

time: 94 us -> 80.2 us (0.85)
  Pallas kernels: 84.2 us -> 70.5 us
    pallas_call x1, Pallas kernels: 77.3 us -> 63.5 us  [body(): pl.pallas_call(functools.partial(exchange_kernel, sizes), out_shape=(jax....]
where the time goes in v3:
time: 80.2 us; the launch traced here: 79.8 us
  Pallas kernels  70.5 us (88%)
  local copies, waits for them, and re-layouts  8.69 us (11%)
    pallas_call x1, Pallas kernels, body(): pl.pallas_call(functools.partial(exchange_kernel, sizes), out_shape=(jax....  63.5 us
    unnamed x22, local copies, waits for them, and re-layouts  8.69 us
    pallas_call x1, Pallas kernels, body(): pl.pallas_call(scatter_kernel, out_shape=(jax.ShapeDtypeStruct((3, rows,...  6.93 us

profile of v3, /device:TPU:1, one launch (start us, length us, event | category | flops | bytes accessed | tf_op | source)
XLA Modules:
  0.0 79.8 jit_solution(18099178380899962520)
XLA Ops:
  0.6 0.0 copy-start.10
  0.6 0.0 copy-start.9
  0.7 0.7 copy-done.10
  1.3 0.0 copy-done.9
  1.3 0.0 copy-start
  1.3 1.0 %copy-done = f32[3,16,16,128]{3,2,1,0:T(8,128)S(1)} copy-done((f32[3,16,16,128]{3,2,1,0:T(8,128)S(1)}, f32[3,16,16,128]{3,2,1,0:T(8,128)}, u32[]{:S(2)}) %copy-start) | copy-done | bytes 393240
  2.3 0.0 copy-start.1
  2.3 1.0 %copy-done.1 = f32[256,3,128]{2,0,1:T(8,128)S(1)} copy-done((f32[256,3,128]{2,0,1:T(8,128)S(1)}, f32[256,3,128]{2,0,1:T(8,128)}, u32[]{:S(2)}) %copy-start.1) | copy-done | bytes 393240
  3.3 0.0 copy-start.2
  3.3 0.9 %copy-done.2 = f32[64,3,128]{2,0,1:T(8,128)S(1)} copy-done((f32[64,3,128]{2,0,1:T(8,128)S(1)}, f32[64,3,128]{2,0,1:T(8,128)}, u32[]{:S(2)}) %copy-start.2) | copy-done | bytes 98328
  4.2 0.0 copy-start.3
  4.2 0.9 %copy-done.3 = f32[16,16,128]{2,1,0:T(8,128)S(1)} copy-done((f32[16,16,128]{2,1,0:T(8,128)S(1)}, f32[16,16,128]{2,1,0:T(8,128)}, u32[]{:S(2)}) %copy-start.3) | copy-done | bytes 131096
  5.1 0.0 copy-start.4
  5.1 0.9 %copy-done.4 = f32[16,16,128]{2,1,0:T(8,128)S(1)} copy-done((f32[16,16,128]{2,1,0:T(8,128)S(1)}, f32[16,16,128]{2,1,0:T(8,128)}, u32[]{:S(2)}) %copy-start.4) | copy-done | bytes 131096
  6.0 0.0 copy-start.5
  6.0 0.9 %copy-done.5 = f32[256,128]{1,0:T(8,128)S(1)} copy-done((f32[256,128]{1,0:T(8,128)S(1)}, f32[256,128]{1,0:T(8,128)}, u32[]{:S(2)}) %copy-start.5) | copy-done | bytes 131096
  6.9 0.0 copy-start.6
  6.9 0.9 %copy-done.6 = s32[256,128]{1,0:T(8,128)S(1)} copy-done((s32[256,128]{1,0:T(8,128)S(1)}, s32[256,128]{1,0:T(8,128)}, u32[]{:S(2)}) %copy-start.6) | copy-done | bytes 131096
  7.8 0.0 copy-start.7
  7.8 0.8 copy-done.7
  8.6 0.0 copy-start.8
  8.6 0.8 copy-done.8
  9.4 63.5 %exchange.1 = (f32[64,24,128]{2,1,0:T(8,128)S(1)}, f32[64,128]{1,0:T(8,128)S(1)}, s32[8,256]{1,0:T(8,128)S(1)}, f32[3,256,128]{2,1,0:T(8,128)S(1)}) custom-call(f32[3,16,16,128]{3,2,1,0:T(8,128)S(1)} %copy-done, f32[16,16,128]{2,1,0:T(8,128)S(1)} %copy-done.3, f32[16,16,128]{2,1,0:T(8,128)S(1)} %copy-done.4, f32[3,256,128]{2,1,0:T(8,128)S(1)} %bitcast.6, ...), custom_call_target="tpu_custom_call" | custom-call | tf_op jit(solution)/shard_map/exchange/pallas_call | solution.py:609
  72.9 6.9 %scatter.1 = (f32[3,256,128]{2,1,0:T(8,128)}, f32[3,256,128]{2,1,0:T(8,128)}) custom-call(f32[64,24,128]{2,1,0:T(8,128)S(1)} %get-tuple-element.8.push, f32[64,128]{1,0:T(8,128)S(1)} %get-tuple-element.9.total, s32[8,256]{1,0:T(8,128)S(1)} %get-tuple-element.10.place, s32[64,128]{1,0:T(8,128)S(1)} %copy-done.7, f32[3,64,128]{2,1,0:T(8,128)S(1)} %bitcast.8, ...), custom_call_target="tpu_custom_call" | custom-call | tf_op jit(solution)/shard_map/scatter/pallas_call | solution.py:675
Async XLA Ops:
  0.6 0.7 copy-start.10
  0.6 0.7 copy-start.9
  1.3 1.0 %copy-start = (f32[3,16,16,128]{3,2,1,0:T(8,128)S(1)}, f32[3,16,16,128]{3,2,1,0:T(8,128)}, u32[]{:S(2)}) copy-start(f32[3,16,16,128]{3,2,1,0:T(8,128)} %refs_0_.1) | copy-start | bytes 1179652
  2.3 1.0 %copy-start.1 = (f32[256,3,128]{2,0,1:T(8,128)S(1)}, f32[256,3,128]{2,0,1:T(8,128)}, u32[]{:S(2)}) copy-start(f32[256,3,128]{2,0,1:T(8,128)} %param.14) | copy-start | bytes 1179652
  3.3 0.9 %copy-start.2 = (f32[64,3,128]{2,0,1:T(8,128)S(1)}, f32[64,3,128]{2,0,1:T(8,128)}, u32[]{:S(2)}) copy-start(f32[64,3,128]{2,0,1:T(8,128)} %param.20) | copy-start | bytes 294916
  4.2 0.9 %copy-start.3 = (f32[16,16,128]{2,1,0:T(8,128)S(1)}, f32[16,16,128]{2,1,0:T(8,128)}, u32[]{:S(2)}) copy-start(f32[16,16,128]{2,1,0:T(8,128)} %refs_1_.1) | copy-start | bytes 393220
  5.1 0.9 %copy-start.4 = (f32[16,16,128]{2,1,0:T(8,128)S(1)}, f32[16,16,128]{2,1,0:T(8,128)}, u32[]{:S(2)}) copy-start(f32[16,16,128]{2,1,0:T(8,128)} %refs_2_.1) | copy-start | bytes 393220
  6.0 0.9 %copy-start.5 = (f32[256,128]{1,0:T(8,128)S(1)}, f32[256,128]{1,0:T(8,128)}, u32[]{:S(2)}) copy-start(f32[256,128]{1,0:T(8,128)} %refs_4_.1) | copy-start | bytes 393220
  6.9 0.9 %copy-start.6 = (s32[256,128]{1,0:T(8,128)S(1)}, s32[256,128]{1,0:T(8,128)}, u32[]{:S(2)}) copy-start(s32[256,128]{1,0:T(8,128)} %refs_5_.1) | copy-start | bytes 393220
  7.8 0.8 copy-start.7
  8.6 0.8 copy-start.8

commit v4 on v3

--- a/solution.py
+++ b/solution.py
@@ -40,7 +40,7 @@
     rows = disp.shape[1] * disp.shape[2]
     for c in range(3):
         turned = jnp.transpose(disp[c].reshape(rows, LANES))
-        for s, part in enumerate(split3(turned)):
+        for s, part in enumerate(split3(turned)[:2]):
             table[c * LANES : (c + 1) * LANES, s * rows : (s + 1) * rows] = part
     row_at = iota((rows, 2 * LANES), 0)
     lane_at = iota((LANES, 2 * LANES), 0)
@@ -48,7 +48,7 @@
     def step(q, carry):
         index = jnp.concatenate([mnode[pl.ds(2 * q + u, 1), :] for u in range(2)], axis=1)
         hot = (lax.shift_right_logical(index, 7) == row_at).astype(f32).astype(bf16)
-        picked = dot(table[...], jnp.concatenate([hot, hot, hot], axis=0))
+        picked = dot(table[...], jnp.concatenate([hot, hot], axis=0))
         here = (index & (LANES - 1)) == lane_at
         for c in range(3):
             row = jnp.sum(
@@ -58,7 +58,7 @@
                 centers[c, pl.ds(2 * q + u, 1), :] = row[:, u * LANES : (u + 1) * LANES]
         return carry
 
-    lax.fori_loop(0, mnode.shape[0] // 2, step, 0, unroll=4)
+    lax.fori_loop(0, mnode.shape[0] // 2, step, 0, unroll=8)
 
 
 def contact_slots(master, slave):
@@ -265,299 +265,23 @@
                 if i > 0:
                     out[c, (i - 1) * cells_y : i * cells_y, :] += (aside - along)[0:cells_y]
             low = high
-
-
-def split_refs(refs, counts):
-    groups, at = [], 0
-    for count in counts:
-        groups.append(refs[at : at + count])
-        at += count
-    return groups
-
-
-def exchange_kernel(sizes, *refs):
-    (
-        inputs,
-        (push_out, total_out, place_out, zone_out),
-        locals_,
-        (ask_send, ask_recv, packs, give_send, give_recv, back_send, back_recv, sum_send, sum_recv),
-        (slave, centers, table, hot, hot_t),
-        (held, y_send, y_recv, z_send, z_recv),
-        (in_sems, ask_sems, ring_sems, give_sems, back_sems, sum_sems, halo_sems),
-    ) = split_refs(refs, (11, 4, 11, 9, 5, 5, 7))
-    disp, mass, energy, spos, sstiff, sactive, peer, block, mnode, marea, factive = locals_
-    size_y, size_z = sizes[1:]
-    peers = size_y * size_z
-    count = peer.shape[1]
-    masters = mnode.shape[0]
-    gx, gy, gz = lax.axis_index("gx"), lax.axis_index("gy"), lax.axis_index("gz")
-    halo = Halo(disp, mass, energy, held, y_send, y_recv, z_send, z_recv, halo_sems, sizes)
-
-    def load(n):
-        return pltpu.make_async_copy(inputs[n], locals_[n], in_sems.at[n])
-
-    for n in range(11):
-        load(n).start()
-
-    def along_y(shift):
-        return (gx, lax.rem(gy + shift + size_y, size_y), gz)
-
-    def along_z(shift):
-        return (gx, gy, lax.rem(gz + shift + size_z, size_z))
-
-    barrier = pltpu.get_barrier_semaphore()
-    greeted = [along_y(n) for n in range(1, size_y)] + [along_z(n) for n in range(1, size_z)]
-    greeted += [halo.beside(0, 1), halo.beside(0, -1)]
-    for device in greeted:
-        pl.semaphore_signal(barrier, inc=1, device_id=device, device_id_type=MESH)
-
-    def z_shift(b):
-        return jnp.where(b % 2 == 1, -((b + 1) // 2), b // 2)
-
-    for n in range(11):
-        load(n).wait()
-
-    named = peer[...]
-    aside = lax.rem(named // size_z - gy + size_y, size_y)
-    away = lax.rem(named % size_z - gz + size_z, size_z)
-    batch = jnp.where(away < size_z // 2, 2 * away, 2 * (size_z - away) - 1)
-    to_peer = (aside * size_z + batch == iota((peers, count), 0)).astype(f32)
-    before = (iota((count, count), 0) < iota((count, count), 1)).astype(f32).astype(bf16)
-    rank = jnp.sum(to_peer * dot(to_peer.astype(bf16), before), axis=0, keepdims=True).astype(i32)
-    place = (batch * size_y + aside) * SLOTS + rank
-    place_out[...] = jnp.broadcast_to(place, place_out.shape)
-    in_rank = jnp.where(rank == iota((LANES, count), 0), (block[...] + 1).astype(f32), 0.0)
-    asked = lax.dot_general(
-        to_peer.astype(bf16), in_rank.astype(bf16), NT, preferred_element_type=f32
-    )
-    for t in range(peers):
-        ask_send[t] = asked[t : t + 1, :]
-    ask_recv[0:size_z] = ask_send[0:size_z]
-
-    pl.semaphore_wait(barrier, len(greeted))
-
-    def ask_copy(n):
-        rows = pl.ds(n * size_z, size_z)
-        return pltpu.make_async_remote_copy(
-            src_ref=ask_send.at[rows],
-            dst_ref=ask_recv.at[rows],
-            send_sem=ask_sems.at[0, n],
-            recv_sem=ask_sems.at[1, n],
-            device_id=along_y(n),
-            device_id_type=MESH,
-        )
-
-    half = masters // 2
-
-    def ring_copy(step, up):
-        side = 0 if up else 1
-        source = 0 if step == 0 else 2 * step - 1 + side
-        target = 2 * step + 1 + side
-        if step == size_z // 2 - 1:
-            rows, target = pl.ds(side * half, half), size_z - 1
-        else:
-            rows = pl.ds(0, masters)
-        return pltpu.make_async_remote_copy(
-            src_ref=packs.at[source, rows],
-            dst_ref=packs.at[target, rows],
-            send_sem=ring_sems.at[0, side, step],
-            recv_sem=ring_sems.at[1, side, step],
-            device_id=along_z(1 if up else -1),
-            device_id_type=MESH,
-        )
-
-    def give_copy(b, n):
-        t = b * size_y + n
-        return pltpu.make_async_remote_copy(
-            src_ref=give_send.at[t],
-            dst_ref=give_recv.at[t],
-            send_sem=give_sems.at[0, t],
-            recv_sem=give_sems.at[1, t],
-            device_id=along_y(-n),
-            device_id_type=MESH,
-        )
-
-    def back_copy(b, n):
-        t = b * size_y + n
-        return pltpu.make_async_remote_copy(
-            src_ref=back_send.at[t],
-            dst_ref=back_recv.at[t],
-            send_sem=back_sems.at[0, t],
-            recv_sem=back_sems.at[1, t],
-            device_id=along_y(n),
-            device_id_type=MESH,
-        )
-
-    def sum_copy(b):
-        return pltpu.make_async_remote_copy(
-            src_ref=sum_send.at[b],
-            dst_ref=sum_recv.at[b],
-            send_sem=sum_sems.at[0, b],
-            recv_sem=sum_sems.at[1, b],
-            device_id=along_z(z_shift(b)),
-            device_id_type=MESH,
-        )
-
-    for n in range(1, size_y):
-        ask_copy(n).start()
-    for copy in halo.x_copies():
-        copy.start()
-    halo.own_part()
-
-    gather_centers(disp, mnode, centers, table)
-    live = factive[...].astype(f32)
-    areas = [marea[c] * live for c in range(3)]
-    moved = areas[0] * centers[0] + areas[1] * centers[1] + areas[2] * centers[2]
-    packs[0] = jnp.concatenate(areas + [moved], axis=1)
-    ring_copy(0, True).start()
-    ring_copy(0, False).start()
-
-    for copy in halo.x_copies():
-        copy.wait_recv()
-    halo.y_start()
-
-    for n in range(1, size_y):
-        ask_copy(n).wait_recv()
-    diagonal = (iota((peers, SLOTS, LANES), 1) == iota((peers, SLOTS, LANES), 2)).astype(f32)
-    wanted = jnp.sum(
-        jnp.broadcast_to(ask_recv[...], (peers, SLOTS, LANES)) * diagonal, axis=2, keepdims=True
-    )
-    picked = (wanted.astype(i32) - 1 == iota((peers, SLOTS, LANES), 2)).astype(f32)
-    hot[...] = picked.reshape(size_y, size_z, SLOTS, LANES)
-    for b in range(size_z):
-        chosen = hot[:, b].reshape(size_y * SLOTS, LANES)
-        hot_t[b] = jnp.transpose(chosen)[0:masters].astype(bf16)
-
-    def give(b):
-        chosen = hot[:, b].reshape(size_y * SLOTS, LANES)[:, 0:masters]
-        chosen = jnp.concatenate([chosen, chosen, chosen], axis=1).astype(bf16)
-        given = dot(chosen, jnp.concatenate(split3(packs[b]), axis=0))
-        for c in range(4):
-            give_send[b * size_y : (b + 1) * size_y, c * SLOTS : (c + 1) * SLOTS, :] = given[
-                :, c * LANES : (c + 1) * LANES
-            ].reshape(size_y, SLOTS, LANES)
-        for n in range(1, size_y):
-            give_copy(b, n).start()
-        give_recv[b * size_y] = give_send[b * size_y]
-
-    give(0)
-    for copy in halo.y_copies():
-        copy.wait_recv()
-    halo.z_start()
-
-    stiff = sstiff[...] * sactive[...].astype(f32)
-    slots = (place == iota((peers * SLOTS, count), 0)).astype(f32).astype(bf16)
-    for c in range(4):
-        field = stiff if c == 3 else -(stiff * spos[c])
-        parts = split3(field)
-        rows = dot(slots, parts[0]) + dot(slots, parts[1]) + dot(slots, parts[2])
-        slave[:, c * SLOTS : (c + 1) * SLOTS, :] = rows.reshape(peers, SLOTS, LANES)
-
-    for copy in halo.z_copies():
-        copy.wait_recv()
-    halo.zone_forces(zone_out)
-
-    def ring_step(step):
-        last = step == size_z // 2 - 1
-        for up in (True, False):
-            ring_copy(step, up).wait_recv()
-            if not last:
-                ring_copy(step + 1, up).start()
-        for b in (2 * step + 1, 2 * step + 2):
-            if b < size_z:
-                give(b)
-
-    def summed(b):
-        for n in range(1, size_y):
-            back_copy(b, n).wait_recv()
-        rows = back_recv[pl.ds(b * size_y, size_y)].reshape(size_y * SLOTS, LANES)
-        parts = split3(rows)
-        turned = hot_t[b]
-        sum_send[b] = dot(turned, parts[0]) + dot(turned, parts[1]) + dot(turned, parts[2])
-
-        @pl.when(b > 0)
-        def _():
-            sum_copy(b).start()
-
-    step_of = 4
-    parts_of = size_y // step_of
-
-    def contact(q, carry):
-        for step in range(size_z // 2):
-
-            @pl.when(q == 3 * step)
-            def _():
-                ring_step(step)
-
-        @pl.when((q % parts_of == 0) & (q >= 2 * parts_of))
-        def _():
-            summed(q // parts_of - 2)
-
-        b = q // parts_of
-        for u in range(step_of):
-            n = (q % parts_of) * step_of + u
-
-            @pl.when(n > 0)
-            def _():
-                give_copy(b, n).wait_recv()
-
-        for u in range(step_of):
-            t = q * step_of + u
-            push, total = contact_slots(give_recv[t], slave[t])
-            push_out[t] = push
-            back_send[t] = total
-        for u in range(step_of):
-            n = (q % parts_of) * step_of + u
-
-            @pl.when(n > 0)
-            def _():
-                back_copy(b, n).start()
-
-            @pl.when(n == 0)
-            def _():
-                back_recv[b * size_y] = back_send[b * size_y]
-
-        return carry
-
-    lax.fori_loop(0, size_z * parts_of, contact, 0)
-    summed(size_z - 2)
-    summed(size_z - 1)
-
-    def sent(b, carry):
-        for n in range(1, size_y):
-            give_copy(b, n).wait_send()
-            back_copy(b, n).wait_send()
-        return carry
-
-    lax.fori_loop(0, size_z, sent, 0)
-    for n in range(1, size_y):
-        ask_copy(n).wait_send()
-    for step in range(size_z // 2):
-        ring_copy(step, True).wait_send()
-        ring_copy(step, False).wait_send()
-    for copy in halo.x_copies() + halo.y_copies() + halo.z_copies():
-        copy.wait_send()
-    total = sum_send[0]
-    for b in range(1, size_z):
-        sum_copy(b).wait_recv()
-        sum_copy(b).wait_send()
-        total = total + sum_recv[b]
-    total_out[...] = total
-
-
-def scatter_kernel(push, total, place, mnode, marea, zone, node_out, slave_out, grid):
-    masters = mnode.shape[0]
-    peers = push.shape[0]
-    count = place.shape[1]
-    rows = zone.shape[1]
-
-    turned = jnp.transpose(place[...])
-    slots = (turned[:, 0:1] == iota((count, peers * SLOTS), 1)).astype(f32).astype(bf16)
+            if i == cells_x // 2:
+                yield
+        yield
+
+
+def slave_forces(push, place, slave_out):
+    count, slots_of = place.shape[1], push.shape[0] * SLOTS
+    turned = jnp.transpose(jnp.broadcast_to(place, (8, count)))
+    slots = (turned[:, 0:1] == iota((count, slots_of), 1)).astype(f32).astype(bf16)
     for c in range(3):
-        field = push[:, c * SLOTS : (c + 1) * SLOTS, :].reshape(peers * SLOTS, LANES)
+        field = push[:, c * SLOTS : (c + 1) * SLOTS, :].reshape(slots_of, LANES)
         parts = split3(field)
         slave_out[c] = dot(slots, parts[0]) + dot(slots, parts[1]) + dot(slots, parts[2])
 
+
+def add_reactions(total, mnode, marea, zone, node_out, grid):
+    masters, rows = mnode.shape[0], zone.shape[1]
     row_at = iota((rows, 2 * LANES), 0)
     lane_at = iota((LANES, 2 * LANES), 0)
     grid[...] = jnp.zeros_like(grid)
@@ -581,9 +305,327 @@
         )
         return carry
 
-    lax.fori_loop(0, masters // 2, step, 0, unroll=4)
+    lax.fori_loop(0, masters // 2, step, 0, unroll=8)
     for c in range(3):
         node_out[c] = zone[c] + jnp.transpose(grid[c * LANES : (c + 1) * LANES, :])
+
+
+def split_refs(refs, counts):
+    groups, at = [], 0
+    for count in counts:
+        groups.append(refs[at : at + count])
+        at += count
+    return groups
+
+
+def exchange_kernel(sizes, *refs):
+    (
+        inputs,
+        (node_out, slave_out),
+        locals_,
+        (ask_send, ask_recv, packs, give_send, give_recv, back_send, back_recv, sum_send, sum_recv),
+        (slave, centers, table, hot, hot_t, push_out, total_out, zone_out, grid),
+        (held, y_send, y_recv, z_send, z_recv),
+        (in_sems, ask_sems, ring_sems, give_sems, back_sems, sum_sems, halo_sems),
+    ) = split_refs(refs, (11, 2, 11, 9, 9, 5, 7))
+    disp, mass, energy, spos, sstiff, sactive, peer, block, mnode, marea, factive = locals_
+    size_y, size_z = sizes[1:]
+    peers = size_y * size_z
+    count = peer.shape[1]
+    masters = mnode.shape[0]
+    gx, gy, gz = lax.axis_index("gx"), lax.axis_index("gy"), lax.axis_index("gz")
+    halo = Halo(disp, mass, energy, held, y_send, y_recv, z_send, z_recv, halo_sems, sizes)
+
+    def load(n):
+        return pltpu.make_async_copy(inputs[n], locals_[n], in_sems.at[n])
+
+    for n in (6, 7, 0, 8, 1, 2, 9, 10, 4, 5, 3):
+        load(n).start()
+
+    def along_y(shift):
+        return (gx, lax.rem(gy + shift + size_y, size_y), gz)
+
+    def along_z(shift):
+        return (gx, gy, lax.rem(gz + shift + size_z, size_z))
+
+    barrier = pltpu.get_barrier_semaphore()
+    greeted = size_y + size_z
+
+    def greet_y(n, carry):
+        pl.semaphore_signal(barrier, inc=1, device_id=along_y(n), device_id_type=MESH)
+        return carry
+
+    def greet_z(n, carry):
+        pl.semaphore_signal(barrier, inc=1, device_id=along_z(n), device_id_type=MESH)
+        return carry
+
+    lax.fori_loop(1, size_y, greet_y, 0)
+    lax.fori_loop(1, size_z, greet_z, 0)
+    for side in (1, -1):
+        pl.semaphore_signal(
+            barrier, inc=1, device_id=halo.beside(0, side), device_id_type=MESH
+        )
+
+    def z_shift(b):
+        return jnp.where(b % 2 == 1, -((b + 1) // 2), b // 2)
+
+    for n in (6, 7):
+        load(n).wait()
+
+    named = peer[...]
+    aside = lax.rem(named // size_z - gy + size_y, size_y)
+    away = lax.rem(named % size_z - gz + size_z, size_z)
+    batch = jnp.where(away < size_z // 2, 2 * away, 2 * (size_z - away) - 1)
+    to_peer = (aside * size_z + batch == iota((peers, count), 0)).astype(f32)
+    before = (iota((count, count), 0) < iota((count, count), 1)).astype(f32).astype(bf16)
+    rank = jnp.sum(to_peer * dot(to_peer.astype(bf16), before), axis=0, keepdims=True).astype(i32)
+    place = (batch * size_y + aside) * SLOTS + rank
+    in_rank = jnp.where(rank == iota((LANES, count), 0), (block[...] + 1).astype(f32), 0.0)
+    asked = lax.dot_general(
+        to_peer.astype(bf16), in_rank.astype(bf16), NT, preferred_element_type=f32
+    )
+    for t in range(peers):
+        ask_send[t] = asked[t : t + 1, :]
+    ask_recv[0:size_z] = ask_send[0:size_z]
+
+    for n in (0, 1, 2):
+        load(n).wait()
+    pl.semaphore_wait(barrier, greeted)
+
+    def ask_copy(n):
+        rows = pl.ds(n * size_z, size_z)
+        return pltpu.make_async_remote_copy(
+            src_ref=ask_send.at[rows],
+            dst_ref=ask_recv.at[rows],
+            send_sem=ask_sems.at[0, n],
+            recv_sem=ask_sems.at[1, n],
+            device_id=along_y(n),
+            device_id_type=MESH,
+        )
+
+    half = masters // 2
+
+    def ring_copy(step, up, chunk):
+        side = 0 if up else 1
+        source = 0 if step == 0 else 2 * step - 1 + side
+        target = 2 * step + 1 + side
+        if step == size_z // 2 - 1:
+            target = size_z - 1
+        rows = pl.ds(chunk * half, half)
+        return pltpu.make_async_remote_copy(
+            src_ref=packs.at[source, rows],
+            dst_ref=packs.at[target, rows],
+            send_sem=ring_sems.at[0, side, step, chunk],
+            recv_sem=ring_sems.at[1, side, step, chunk],
+            device_id=along_z(1 if up else -1),
+            device_id_type=MESH,
+        )
+
+    def ring_copies(step):
+        if step == size_z // 2 - 1:
+            return [(True, 0), (False, 1)]
+        return [(True, 0), (False, 1), (True, 1), (False, 0)]
+
+    def give_copy(b, n):
+        t = b * size_y + n
+        return pltpu.make_async_remote_copy(
+            src_ref=give_send.at[t],
+            dst_ref=give_recv.at[t],
+            send_sem=give_sems.at[0, t],
+            recv_sem=give_sems.at[1, t],
+            device_id=along_y(-n),
+            device_id_type=MESH,
+        )
+
+    def back_copy(b, n):
+        t = b * size_y + n
+        return pltpu.make_async_remote_copy(
+            src_ref=back_send.at[t],
+            dst_ref=back_recv.at[t],
+            send_sem=back_sems.at[0, t],
+            recv_sem=back_sems.at[1, t],
+            device_id=along_y(n),
+            device_id_type=MESH,
+        )
+
+    def sum_copy(b):
+        return pltpu.make_async_remote_copy(
+            src_ref=sum_send.at[b],
+            dst_ref=sum_recv.at[b],
+            send_sem=sum_sems.at[0, b],
+            recv_sem=sum_sems.at[1, b],
+            device_id=along_z(z_shift(b)),
+            device_id_type=MESH,
+        )
+
+    def each(n, carry):
+        ask_copy(n).start()
+        return carry
+
+    lax.fori_loop(1, size_y, each, 0)
+    for copy in halo.x_copies():
+        copy.start()
+    for n in (8, 9, 10):
+        load(n).wait()
+    gather_centers(disp, mnode, centers, table)
+    live = factive[...].astype(f32)
+    areas = [marea[c] * live for c in range(3)]
+    moved = areas[0] * centers[0] + areas[1] * centers[1] + areas[2] * centers[2]
+    packs[0] = jnp.concatenate(areas + [moved], axis=1)
+    for way in ring_copies(0):
+        ring_copy(0, *way).start()
+
+    def each(n, carry):
+        ask_copy(n).wait_recv()
+        return carry
+
+    lax.fori_loop(1, size_y, each, 0)
+    diagonal = (iota((peers, SLOTS, LANES), 1) == iota((peers, SLOTS, LANES), 2)).astype(f32)
+    wanted = jnp.sum(
+        jnp.broadcast_to(ask_recv[...], (peers, SLOTS, LANES)) * diagonal, axis=2, keepdims=True
+    )
+    picked = (wanted.astype(i32) - 1 == iota((peers, SLOTS, LANES), 2)).astype(f32)
+    hot[...] = picked.reshape(size_y, size_z, SLOTS, LANES)
+    for b in range(size_z):
+        chosen = hot[:, b].reshape(size_y * SLOTS, LANES)
+        hot_t[b] = jnp.transpose(chosen)[0:masters].astype(bf16)
+
+    def give(b):
+        chosen = hot[:, b].reshape(size_y * SLOTS, LANES)[:, 0:masters]
+        chosen = jnp.concatenate([chosen, chosen, chosen], axis=1).astype(bf16)
+        given = dot(chosen, jnp.concatenate(split3(packs[b]), axis=0))
+        for c in range(4):
+            give_send[b * size_y : (b + 1) * size_y, c * SLOTS : (c + 1) * SLOTS, :] = given[
+                :, c * LANES : (c + 1) * LANES
+            ].reshape(size_y, SLOTS, LANES)
+        def each(n, carry):
+            give_copy(b, n).start()
+            return carry
+
+        lax.fori_loop(1, size_y, each, 0)
+        give_recv[b * size_y] = give_send[b * size_y]
+
+    give(0)
+    halo.own_part()
+    for copy in halo.x_copies():
+        copy.wait_recv()
+    halo.y_start()
+    for n in (3, 4, 5):
+        load(n).wait()
+
+    stiff = sstiff[...] * sactive[...].astype(f32)
+    slots = (place == iota((peers * SLOTS, count), 0)).astype(f32).astype(bf16)
+    for c in range(4):
+        field = stiff if c == 3 else -(stiff * spos[c])
+        parts = split3(field)
+        rows = dot(slots, parts[0]) + dot(slots, parts[1]) + dot(slots, parts[2])
+        slave[:, c * SLOTS : (c + 1) * SLOTS, :] = rows.reshape(peers, SLOTS, LANES)
+
+    for copy in halo.y_copies():
+        copy.wait_recv()
+    halo.z_start()
+
+    def ring_step(step):
+        for way in ring_copies(step):
+            ring_copy(step, *way).wait_recv()
+            if step < size_z // 2 - 1 and way in ring_copies(step + 1):
+                ring_copy(step + 1, *way).start()
+        for b in (2 * step + 1, 2 * step + 2):
+            if b < size_z:
+                give(b)
+
+    def summed(b):
+        def each(n, carry):
+            back_copy(b, n).wait_recv()
+            return carry
+
+        lax.fori_loop(1, size_y, each, 0)
+        rows = back_recv[pl.ds(b * size_y, size_y)].reshape(size_y * SLOTS, LANES)
+        parts = split3(rows)
+        turned = hot_t[b]
+        sum_send[b] = dot(turned, parts[0]) + dot(turned, parts[1]) + dot(turned, parts[2])
+
+        @pl.when(b > 0)
+        def _():
+            sum_copy(b).start()
+
+    step_of = 4
+    parts_of = size_y // step_of
+
+    def contact(q, carry):
+        for step in range(size_z // 2):
+
+            @pl.when(q == 3 * step)
+            def _():
+                ring_step(step)
+
+        @pl.when((q % parts_of == 0) & (q >= 2 * parts_of))
+        def _():
+            summed(q // parts_of - 2)
+
+        b = q // parts_of
+        for u in range(step_of):
+            n = (q % parts_of) * step_of + u
+
+            @pl.when(n > 0)
+            def _():
+                give_copy(b, n).wait_recv()
+
+        for u in range(step_of):
+            t = q * step_of + u
+            push, total = contact_slots(give_recv[t], slave[t])
+            push_out[t] = push
+            back_send[t] = total
+        for u in range(step_of):
+            n = (q % parts_of) * step_of + u
+
+            @pl.when(n > 0)
+            def _():
+                back_copy(b, n).start()
+
+            @pl.when(n == 0)
+            def _():
+                back_recv[b * size_y] = back_send[b * size_y]
+
+        return carry
+
+    lax.fori_loop(0, size_z * parts_of, contact, 0)
+    summed(size_z - 2)
+    for copy in halo.z_copies():
+        copy.wait_recv()
+    forces = halo.zone_forces(zone_out)
+    next(forces)
+    slave_forces(push_out, place, slave_out)
+    summed(size_z - 1)
+    next(forces)
+
+    def sent(b, carry):
+        def each(n, carry):
+            give_copy(b, n).wait_send()
+            back_copy(b, n).wait_send()
+            return carry
+
+        lax.fori_loop(1, size_y, each, 0)
+        return carry
+
+    lax.fori_loop(0, size_z, sent, 0)
+    def each(n, carry):
+        ask_copy(n).wait_send()
+        return carry
+
+    lax.fori_loop(1, size_y, each, 0)
+    for step in range(size_z // 2):
+        for way in ring_copies(step):
+            ring_copy(step, *way).wait_send()
+    for copy in halo.x_copies() + halo.y_copies() + halo.z_copies():
+        copy.wait_send()
+    total = sum_send[0]
+    for b in range(1, size_z):
+        sum_copy(b).wait_recv()
+        sum_copy(b).wait_send()
+        total = total + sum_recv[b]
+    total_out[...] = total
+    add_reactions(total_out, mnode, marea, zone_out, node_out, grid)
 
 
 def body(
@@ -606,16 +648,14 @@
     cells = displacement.shape[1:]
     rows = cells[0] * cells[1]
     area = jnp.transpose(master_area, (1, 0, 2))
-    push, total, place, zone = pl.pallas_call(
+    node_force, slave_force = pl.pallas_call(
         functools.partial(exchange_kernel, sizes),
         out_shape=(
-            jax.ShapeDtypeStruct((peers, 24, LANES), f32),
-            jax.ShapeDtypeStruct((masters, LANES), f32),
-            jax.ShapeDtypeStruct((8, count), i32),
             jax.ShapeDtypeStruct((3, rows, LANES), f32),
+            jax.ShapeDtypeStruct((3, count, LANES), f32),
         ),
         in_specs=[HBM] * 11,
-        out_specs=(VMEM,) * 4,
+        out_specs=(VMEM,) * 2,
         scratch_shapes=[
             pltpu.VMEM(displacement.shape, f32),
             pltpu.VMEM(zone_mass.shape, f32),
@@ -639,9 +679,13 @@
             pltpu.VMEM((sizes[2], masters, LANES), f32),
             pltpu.VMEM((peers, 32, LANES), f32),
             pltpu.VMEM((3, masters, LANES), f32),
-            pltpu.VMEM((3 * LANES, 3 * rows), bf16),
+            pltpu.VMEM((3 * LANES, 2 * rows), bf16),
             pltpu.VMEM((sizes[1], sizes[2], SLOTS, LANES), f32),
             pltpu.VMEM((sizes[2], masters, sizes[1] * SLOTS), bf16),
+            pltpu.VMEM((peers, 24, LANES), f32),
+            pltpu.VMEM((masters, LANES), f32),
+            pltpu.VMEM((3, rows, LANES), f32),
+            pltpu.VMEM((3 * LANES, rows), f32),
             pltpu.VMEM((5, cells[0] + 2, cells[1] + 8, LANES), f32),
             pltpu.VMEM((8, cells[0] + 8, LANES), f32),
             pltpu.VMEM((8, cells[0] + 8, LANES), f32),
@@ -649,14 +693,14 @@
             pltpu.VMEM((2, cells[1] + 8, LANES), f32),
             pltpu.SemaphoreType.DMA((11,)),
             pltpu.SemaphoreType.DMA((2, sizes[1])),
-            pltpu.SemaphoreType.DMA((2, 2, sizes[2] // 2)),
+            pltpu.SemaphoreType.DMA((2, 2, sizes[2] // 2, 2)),
             pltpu.SemaphoreType.DMA((2, peers)),
             pltpu.SemaphoreType.DMA((2, peers)),
             pltpu.SemaphoreType.DMA((2, sizes[2])),
             pltpu.SemaphoreType.DMA((2, 8)),
         ],
         compiler_params=pltpu.CompilerParams(
-            collective_id=0, has_side_effects=True, vmem_limit_bytes=48 * 2**20
+            collective_id=0, has_side_effects=True, vmem_limit_bytes=63 * 2**20
         ),
         name="exchange",
     )(
@@ -672,18 +716,6 @@
         area,
         face_active,
     )
-    node_force, slave_force = pl.pallas_call(
-        scatter_kernel,
-        out_shape=(
-            jax.ShapeDtypeStruct((3, rows, LANES), f32),
-            jax.ShapeDtypeStruct((3, count, LANES), f32),
-        ),
-        in_specs=[VMEM] * 6,
-        out_specs=(VMEM,) * 2,
-        scratch_shapes=[pltpu.VMEM((3 * LANES, rows), f32)],
-        compiler_params=pltpu.CompilerParams(vmem_limit_bytes=48 * 2**20),
-        name="scatter",
-    )(push, total, place, master_node, area, zone)
     return (
         node_force.reshape((3,) + cells),
         jnp.transpose(slave_force, (1, 0, 2)),

time: 80.2 us -> 64.8 us (0.81)
  Pallas kernels: 70.5 us -> 61.4 us
  local copies, waits for them, and re-layouts: 8.69 us -> 2.57 us
    pallas_call x1 -> x0, Pallas kernels: 6.93 us -> none  [body(): pl.pallas_call(scatter_kernel, out_shape=(jax.ShapeDtypeStruct((3, rows,...]
    unnamed x22 -> x4, local copies, waits for them, and re-layouts: 8.69 us -> 2.57 us
    pallas_call x1, Pallas kernels: 63.5 us -> 61.4 us  [body(): pl.pallas_call(functools.partial(exchange_kernel, sizes), out_shape=(jax....]
where the time goes in v4:
time: 64.8 us; the launch traced here: 64.7 us
  Pallas kernels  61.4 us (95%)
  local copies, waits for them, and re-layouts  2.57 us (4%)
  between operations  0.65 us (1%)
    pallas_call x1, Pallas kernels, body(): pl.pallas_call(functools.partial(exchange_kernel, sizes), out_shape=(jax....  61.4 us
    unnamed x4, local copies, waits for them, and re-layouts  2.57 us

profile of v4, /device:TPU:1, one launch (start us, length us, event | category | flops | bytes accessed | tf_op | source)
XLA Modules:
  0.0 64.7 jit_solution(1578511522583850732)
XLA Ops:
  0.6 61.4 %exchange.1 = (f32[3,256,128]{2,1,0:T(8,128)}, f32[3,256,128]{2,1,0:T(8,128)}) custom-call(f32[3,16,16,128]{3,2,1,0:T(8,128)} %refs_0_.1, f32[16,16,128]{2,1,0:T(8,128)} %refs_1_.1, f32[16,16,128]{2,1,0:T(8,128)} %refs_2_.1, f32[3,256,128]{2,1,0:T(8,128)} %bitcast.8, f32[256,128]{1,0:T(8,128)} %refs_4_.1, s32[256,128]{1,0:T(8,128)} %refs_5_.1, ...), custom_call_target="tpu_custom_call" | custom-call | tf_op jit(solution)/shard_map/exchange/pallas_call | solution.py:651
  62.1 0.0 copy-start
  62.1 1.8 %copy.15 = f32[3,16,16,128]{3,2,1,0:T(8,128)} copy(f32[3,16,16,128]{3,2,1,0:T(8,128)} %bitcast.7) | data formatting | bytes 786432
  63.9 0.0 copy-done
  63.9 0.7 %copy.16 = f32[256,3,128]{2,0,1:T(8,128)} copy(f32[256,3,128]{2,0,1:T(8,128)S(1)} %bitcast.6) | data formatting | bytes 786432
Async XLA Ops:
  62.1 1.8 %copy-start = (f32[3,256,128]{2,1,0:T(8,128)S(1)}, f32[3,256,128]{2,1,0:T(8,128)}, u32[]{:S(2)}) copy-start(f32[3,256,128]{2,1,0:T(8,128)} %get-tuple-element.5) | copy-start | bytes 1179652

commit v5 on v4

--- a/solution.py
+++ b/solution.py
@@ -73,25 +73,28 @@
         axis=1,
     ).astype(bf16)
     weights = jnp.concatenate([s1, s1, s1, s2, s2, s3, zero, zero], axis=0)
-    slot_row = iota((256, LANES), 0) & (SLOTS - 1)
-    areas = jnp.concatenate([m1[:24], zero[:8], m2[:24], zero[:8]], axis=0).astype(bf16)
-    areas = jnp.concatenate([areas, areas], axis=1)
-    push_row = iota((64, LANES), 0) & (SLOTS - 1)
-    push = jnp.zeros((64, LANES), f32)
-    columns = []
+    slot_of_row = lax.shift_right_logical(iota((256, LANES), 0), 2) & (SLOTS - 1)
+    first = iota((8, LANES), 0) < 4
+    pushes, columns = [], []
     for q in range(SLOTS // 2):
         chosen = jnp.concatenate(
-            [jnp.where(slot_row == 2 * q + u, weights, 0.0).astype(bf16) for u in range(2)], axis=1
+            [jnp.where(slot_of_row == 2 * q + u, weights, 0.0).astype(bf16) for u in range(2)],
+            axis=1,
         )
         depth = jnp.maximum(dot(turned, chosen), 0.0)
         high = depth.astype(bf16)
         low = (depth - high.astype(f32)).astype(bf16)
-        sums = dot(areas, jnp.concatenate([high, low], axis=0))
+        pair = slice(8 * q, 8 * q + 8)
+        areas = jnp.concatenate([m1[pair], m2[pair]], axis=0).astype(bf16)
+        sums = dot(
+            jnp.concatenate([areas, areas], axis=1), jnp.concatenate([high, low], axis=0)
+        )
+        both = sums[0:8] + sums[8:16]
+        pushes.append(jnp.where(first, both[:, 0:LANES], both[:, LANES : 2 * LANES]))
         for u in range(2):
             half = slice(u * LANES, (u + 1) * LANES)
-            push = jnp.where(push_row == 2 * q + u, sums[:, half], push)
             columns.append(jnp.sum(depth[:, half], axis=1, keepdims=True))
-    return push[:24] + push[32:56], jnp.transpose(jnp.concatenate(columns, axis=1))
+    return jnp.concatenate(pushes, axis=0), jnp.transpose(jnp.concatenate(columns, axis=1))
 
 
 def cross_parts(left, right):
@@ -275,7 +278,7 @@
     turned = jnp.transpose(jnp.broadcast_to(place, (8, count)))
     slots = (turned[:, 0:1] == iota((count, slots_of), 1)).astype(f32).astype(bf16)
     for c in range(3):
-        field = push[:, c * SLOTS : (c + 1) * SLOTS, :].reshape(slots_of, LANES)
+        field = push[:, pl.ds(c, SLOTS, stride=4), :].reshape(slots_of, LANES)
         parts = split3(field)
         slave_out[c] = dot(slots, parts[0]) + dot(slots, parts[1]) + dot(slots, parts[2])
 
@@ -495,7 +498,7 @@
         chosen = jnp.concatenate([chosen, chosen, chosen], axis=1).astype(bf16)
         given = dot(chosen, jnp.concatenate(split3(packs[b]), axis=0))
         for c in range(4):
-            give_send[b * size_y : (b + 1) * size_y, c * SLOTS : (c + 1) * SLOTS, :] = given[
+            give_send[b * size_y : (b + 1) * size_y, pl.ds(c, SLOTS, stride=4), :] = given[
                 :, c * LANES : (c + 1) * LANES
             ].reshape(size_y, SLOTS, LANES)
         def each(n, carry):
@@ -519,7 +522,7 @@
         field = stiff if c == 3 else -(stiff * spos[c])
         parts = split3(field)
         rows = dot(slots, parts[0]) + dot(slots, parts[1]) + dot(slots, parts[2])
-        slave[:, c * SLOTS : (c + 1) * SLOTS, :] = rows.reshape(peers, SLOTS, LANES)
+        slave[:, pl.ds(c, SLOTS, stride=4), :] = rows.reshape(peers, SLOTS, LANES)
 
     for copy in halo.y_copies():
         copy.wait_recv()
@@ -682,7 +685,7 @@
             pltpu.VMEM((3 * LANES, 2 * rows), bf16),
             pltpu.VMEM((sizes[1], sizes[2], SLOTS, LANES), f32),
             pltpu.VMEM((sizes[2], masters, sizes[1] * SLOTS), bf16),
-            pltpu.VMEM((peers, 24, LANES), f32),
+            pltpu.VMEM((peers, 32, LANES), f32),
             pltpu.VMEM((masters, LANES), f32),
             pltpu.VMEM((3, rows, LANES), f32),
             pltpu.VMEM((3 * LANES, rows), f32),

time: 64.8 us -> 64.5 us (level)
  no operation moved by 1% of the time
where the time goes in v5:
time: 64.5 us; the launch traced here: 64.4 us
  Pallas kernels  61.1 us (95%)
  local copies, waits for them, and re-layouts  2.57 us (4%)
  between operations  0.65 us (1%)
    pallas_call x1, Pallas kernels, body(): pl.pallas_call(functools.partial(exchange_kernel, sizes), out_shape=(jax....  61.1 us
    unnamed x4, local copies, waits for them, and re-layouts  2.57 us

profile of v5, /device:TPU:1, one launch (start us, length us, event | category | flops | bytes accessed | tf_op | source)
XLA Modules:
  0.0 64.4 jit_solution(16642237709648924297)
XLA Ops:
  0.6 61.1 %exchange.1 = (f32[3,256,128]{2,1,0:T(8,128)}, f32[3,256,128]{2,1,0:T(8,128)}) custom-call(f32[3,16,16,128]{3,2,1,0:T(8,128)} %refs_0_.1, f32[16,16,128]{2,1,0:T(8,128)} %refs_1_.1, f32[16,16,128]{2,1,0:T(8,128)} %refs_2_.1, f32[3,256,128]{2,1,0:T(8,128)} %bitcast.8, f32[256,128]{1,0:T(8,128)} %refs_4_.1, s32[256,128]{1,0:T(8,128)} %refs_5_.1, ...), custom_call_target="tpu_custom_call" | custom-call | tf_op jit(solution)/shard_map/exchange/pallas_call | solution.py:654
  61.8 0.0 copy-start
  61.8 1.8 %copy.15 = f32[3,16,16,128]{3,2,1,0:T(8,128)} copy(f32[3,16,16,128]{3,2,1,0:T(8,128)} %bitcast.7) | data formatting | bytes 786432
  63.6 0.0 copy-done
  63.6 0.7 %copy.16 = f32[256,3,128]{2,0,1:T(8,128)} copy(f32[256,3,128]{2,0,1:T(8,128)S(1)} %bitcast.6) | data formatting | bytes 786432
Async XLA Ops:
  61.8 1.8 %copy-start = (f32[3,256,128]{2,1,0:T(8,128)S(1)}, f32[3,256,128]{2,1,0:T(8,128)}, u32[]{:S(2)}) copy-start(f32[3,256,128]{2,1,0:T(8,128)} %get-tuple-element.5) | copy-start | bytes 1179652
